TPU v7x, 32 devices: a whole 2x2x4 slice. The times are simulated.
32 devices in a mesh: dp: 16 (over z, x, core), mp: 2 (over y).
Axes of the slice: x: 2, y: 2, z: 4, core: 2. Of those that a mesh axis runs over, the one named last changes fastest.
Arguments:
- inputs: bfloat16 [16, 1024, 512], P('dp'), may hold values from -6 to 6
- segment_ids: int32 [16, 1024], P('dp'), may hold values from 0 to 3, never falling along the last dimension, each value on 1 to 512 neighbouring positions
- attention_norm_scale: float32 [512], replicated, may hold values from 0.25 to 1.75
- attention_norm_bias: float32 [512], replicated, may hold values from -3 to 3
- qkv_weight: bfloat16 [512, 8, 192], P(None, 'mp'), may hold values from -0.25 to 0.25
- qkv_bias: float32 [8, 192], P('mp'), may hold values from -3 to 3
- out_weight: bfloat16 [8, 64, 512], P('mp'), may hold values from -1 to 1
- out_bias: float32 [512], replicated, may hold values from -3 to 3
- feedforward_norm_scale: float32 [512], replicated, may hold values from 0.25 to 1.75
- feedforward_norm_bias: float32 [512], replicated, may hold values from -3 to 3
- in_weight: bfloat16 [512, 2048], P(None, 'mp'), may hold values from -0.25 to 0.25
- in_bias: float32 [2048], P('mp'), may hold values from -3 to 3
- down_weight: bfloat16 [2048, 512], P('mp'), may hold values from -0.125 to 0.125
- down_bias: float32 [512], replicated, may hold values from -3 to 3
- cotangent: bfloat16 [16, 1024, 512], P('dp'), may hold values from -6 to 6
Outputs:
- outputs: float32 [16, 1024, 512], P('dp', 'mp')
- input_grad: float32 [16, 1024, 512], P('dp', 'mp')
- attn_norm_gain_grad: float32 [512], replicated
- attn_norm_shift_grad: float32 [512], replicated
- qkv_weight_grad: float32 [512, 8, 192], P(None, 'mp')
- qkv_bias_grad: float32 [8, 192], P('mp')
- out_weight_grad: float32 [8, 64, 512], P('mp')
- out_bias_grad: float32 [512], replicated
- ffn_norm_gain_grad: float32 [512], replicated
- ffn_norm_shift_grad: float32 [512], replicated
- in_weight_grad: float32 [512, 2048], P(None, 'mp')
- in_bias_grad: float32 [2048], P('mp')
- down_weight_grad: float32 [2048, 512], P('mp')
- down_bias_grad: float32 [512], replicated
Inputs may be any that keep to these rules, and one draw needn't show every extreme that they name: `segment_ids`: in each row the ids never fall and every gene has 1 to 512 codons; in every draw some gene has exactly 512.
All inputs are finite; a program needn't handle non-finite values.
Results may differ from a plain program's by a relative error of at most 0.019.
Values may be sent and summed in bfloat16 or wider, within the bound.
A program may use at most 128 MiB of HBM per device.

v0:
```python
import math

import jax
import jax.numpy as jnp
from jax import lax
from jax.sharding import PartitionSpec as P

EPS = 1e-05
NEG = -1e30


def normalize_rows(values):
    centered = values - jnp.mean(values, -1, keepdims=True)
    return centered * lax.rsqrt(jnp.mean(centered * centered, -1, keepdims=True) + EPS)


def gelu_exact(values):
    return jax.nn.gelu(values, approximate=False)


def rotate(vectors, count):
    half_size = vectors.shape[-1] // 2
    freq_index = jnp.arange(half_size, dtype=jnp.float32)
    frequency = jnp.exp(freq_index * (-math.log(10000.0) / half_size))
    angles = jnp.arange(count, dtype=jnp.float32)[:, None] * frequency[None, :]
    cosine = jnp.cos(angles)[:, None, :]
    sines = jnp.sin(angles)[:, None, :]
    lower_half = vectors[..., :half_size]
    upper_half = vectors[..., half_size:]
    return jnp.concatenate(
        [lower_half * cosine - upper_half * sines, upper_half * cosine + lower_half * sines], -1
    )


def arrange(projected):
    head_size = projected.shape[-1] // 3
    count = projected.shape[1]
    queries = rotate(projected[..., :head_size], count) * head_size ** (-0.5)
    rotated_keys = rotate(projected[..., head_size : 2 * head_size], count)
    return (queries, rotated_keys, projected[..., 2 * head_size :])


def block_scores(query_block, key_row, seg_block, seg_row):
    scores = jnp.einsum("qhe,khe->hqk", query_block, key_row, preferred_element_type=jnp.float32)
    same_gene = (seg_block[:, None] == seg_row[None, :])[None]
    return jnp.where(same_gene, scores, NEG)


def attend_rows(queries, rotated_keys, values, segment_ids, block_rows):
    seq_length = queries.shape[1]
    block_count = seq_length // block_rows

    def one_row(row_args):
        query_row, key_row, value_row, seg_row = row_args

        def one_block(block_start):
            query_block = lax.dynamic_slice_in_dim(query_row, block_start, block_rows, 0)
            seg_block = lax.dynamic_slice_in_dim(seg_row, block_start, block_rows, 0)
            scores = block_scores(query_block, key_row, seg_block, seg_row)
            row_max = jnp.max(scores, -1, keepdims=True)
            exp_scores = jnp.exp(scores - row_max)
            row_total = jnp.sum(exp_scores, -1, keepdims=True)
            probability = (exp_scores / row_total).astype(jnp.bfloat16)
            block_out = jnp.einsum(
                "hqk,khe->qhe", probability, value_row, preferred_element_type=jnp.float32
            )
            return (block_out, (row_max + jnp.log(row_total))[..., 0])

        starts = jnp.arange(block_count, dtype=jnp.int32) * block_rows
        block_outs, log_totals = lax.map(one_block, starts)
        return (block_outs.reshape(seq_length, query_row.shape[1], query_row.shape[2]), log_totals)

    return lax.map(one_row, (queries, rotated_keys, values, segment_ids))


def attend_back(queries, rotated_keys, values, segment_ids, log_totals, grad_attended, block_rows):
    seq_length = queries.shape[1]
    block_count = seq_length // block_rows

    def one_row(row_args):
        query_row, key_row, value_row, seg_row, total_row, grad_row = row_args

        def one_block(carry, block_index):
            key_acc, value_acc = carry
            block_start = block_index * block_rows
            query_block = lax.dynamic_slice_in_dim(query_row, block_start, block_rows, 0)
            seg_block = lax.dynamic_slice_in_dim(seg_row, block_start, block_rows, 0)
            grad_block = lax.dynamic_slice_in_dim(grad_row, block_start, block_rows, 0)
            scores = block_scores(query_block, key_row, seg_block, seg_row)
            probability = jnp.exp(scores - total_row[block_index][..., None])
            grad_prob = jnp.einsum(
                "qhe,khe->hqk", grad_block, value_row, preferred_element_type=jnp.float32
            )
            delta = jnp.sum(probability * grad_prob, -1, keepdims=True)
            grad_scores = (probability * (grad_prob - delta)).astype(jnp.bfloat16)
            grad_query = jnp.einsum(
                "hqk,khe->qhe", grad_scores, key_row, preferred_element_type=jnp.float32
            )
            key_acc = key_acc + jnp.einsum(
                "hqk,qhe->khe", grad_scores, query_block, preferred_element_type=jnp.float32
            )
            value_acc = value_acc + jnp.einsum(
                "hqk,qhe->khe",
                probability.astype(jnp.bfloat16),
                grad_block,
                preferred_element_type=jnp.float32,
            )
            return ((key_acc, value_acc), grad_query)

        zeros_init = jnp.zeros(key_row.shape, jnp.float32)
        (grad_key, grad_value), grad_queries = lax.scan(
            one_block, (zeros_init, zeros_init), jnp.arange(block_count, dtype=jnp.int32)
        )
        return (grad_queries.reshape(key_row.shape), grad_key, grad_value)

    return lax.map(one_row, (queries, rotated_keys, values, segment_ids, log_totals, grad_attended))


def contract_rows(left, right):
    return lax.dot_general(
        left, right, (((0,), (0,)), ((), ())), preferred_element_type=jnp.float32
    )


def contract_cols(left, right):
    return lax.dot_general(
        left, right, (((1,), (1,)), ((), ())), preferred_element_type=jnp.float32
    )


def local(
    inputs,
    segment_ids,
    attention_norm_scale,
    attention_norm_bias,
    qkv_weight,
    qkv_bias,
    out_weight,
    out_bias,
    feedforward_norm_scale,
    feedforward_norm_bias,
    in_weight,
    in_bias,
    down_weight,
    down_bias,
    cotangent,
):
    row_count, seq_length, model_width = inputs.shape
    head_count = qkv_weight.shape[1]
    triple_size = qkv_weight.shape[2]
    head_size = triple_size // 3
    token_count = row_count * seq_length
    block_rows = min(512, seq_length)
    share_rows = seq_length // lax.axis_size("mp")
    share_start = lax.axis_index("mp") * share_rows

    def select_portion(array):
        return lax.dynamic_slice_in_dim(array, share_start, share_rows, 1)

    layer_input_rows = inputs.astype(jnp.float32)
    first_centered_scaled, first_deviation_backward = jax.vjp(normalize_rows, layer_input_rows)
    normed_reduced_precision = (
        first_centered_scaled * attention_norm_scale + attention_norm_bias
    ).astype(jnp.bfloat16)
    flat_normed = normed_reduced_precision.reshape(token_count, model_width)
    qkv_flat = qkv_weight.reshape(model_width, head_count * triple_size)
    projected = jnp.dot(flat_normed, qkv_flat, preferred_element_type=jnp.float32)
    projected = projected.reshape(row_count, seq_length, head_count, triple_size) + qkv_bias
    (queries, rotated_keys, values), arrange_pull = jax.vjp(arrange, projected)
    query_low = queries.astype(jnp.bfloat16)
    key_low = rotated_keys.astype(jnp.bfloat16)
    value_low = values.astype(jnp.bfloat16)
    attended, log_totals = attend_rows(query_low, key_low, value_low, segment_ids, block_rows)
    flat_attended = attended.astype(jnp.bfloat16).reshape(token_count, head_count * head_size)
    out_flat = out_weight.reshape(head_count * head_size, model_width)
    attn_part = jnp.dot(flat_attended, out_flat, preferred_element_type=jnp.float32)
    attn_part = attn_part.reshape(row_count, seq_length, model_width)
    attn_summed = lax.psum(attn_part, "mp")
    hidden_after_attention = layer_input_rows + attn_summed + out_bias
    second_centered_scaled, second_deviation_backward = jax.vjp(
        normalize_rows, hidden_after_attention
    )
    second_normed_rows = (
        second_centered_scaled * feedforward_norm_scale + feedforward_norm_bias
    ).astype(jnp.bfloat16)
    flat_two = second_normed_rows.reshape(token_count, model_width)
    hidden = jnp.dot(flat_two, in_weight, preferred_element_type=jnp.float32) + in_bias
    active, gelu_pull = jax.vjp(gelu_exact, hidden)
    active_low = active.astype(jnp.bfloat16)
    ffn_part = jnp.dot(active_low, down_weight, preferred_element_type=jnp.float32)
    ffn_part = ffn_part.reshape(row_count, seq_length, model_width)
    ffn_summed = lax.psum(ffn_part.astype(jnp.bfloat16), "mp").astype(jnp.float32)
    outputs = select_portion(hidden_after_attention + ffn_summed + down_bias)
    upstream = cotangent.astype(jnp.float32)
    flat_upstream = cotangent.reshape(token_count, model_width)
    down_bias_grad = jnp.sum(flat_upstream, 0, dtype=jnp.float32)
    down_weight_grad = contract_rows(active_low, flat_upstream)
    grad_active = contract_cols(flat_upstream, down_weight)
    grad_hidden = gelu_pull(grad_active)[0].astype(jnp.bfloat16)
    in_bias_grad = jnp.sum(grad_hidden, 0, dtype=jnp.float32)
    in_weight_grad = contract_rows(flat_two, grad_hidden)
    norm_two_part = contract_cols(grad_hidden, in_weight).reshape(
        row_count, seq_length, model_width
    )
    grad_normed_two = lax.psum(norm_two_part, "mp")
    grad_middle = upstream + second_deviation_backward(grad_normed_two * feedforward_norm_scale)[0]
    grad_branch = grad_middle.astype(jnp.bfloat16)
    second_norm_portion = select_portion(grad_normed_two)
    second_centered_portion = select_portion(second_centered_scaled)
    flat_branch = grad_branch.reshape(token_count, model_width)
    out_bias_grad = jnp.sum(flat_branch, 0, dtype=jnp.float32)
    out_weight_grad = contract_rows(flat_attended, flat_branch).reshape(
        head_count, head_size, model_width
    )
    grad_attended = contract_cols(flat_branch, out_flat).astype(jnp.bfloat16)
    grad_attended = grad_attended.reshape(row_count, seq_length, head_count, head_size)
    grad_query, grad_key, grad_value = attend_back(
        query_low, key_low, value_low, segment_ids, log_totals, grad_attended, block_rows
    )
    grad_projected = arrange_pull((grad_query, grad_key, grad_value))[0].astype(jnp.bfloat16)
    flat_projected = grad_projected.reshape(token_count, head_count * triple_size)
    qkv_bias_grad = jnp.sum(flat_projected, 0, dtype=jnp.float32).reshape(head_count, triple_size)
    qkv_weight_grad = contract_rows(flat_normed, flat_projected).reshape(
        model_width, head_count, triple_size
    )
    norm_one_part = contract_cols(flat_projected, qkv_flat).reshape(
        row_count, seq_length, model_width
    )
    grad_normed_one = lax.psum(norm_one_part.astype(jnp.bfloat16), "mp").astype(jnp.float32)
    input_grad = select_portion(
        grad_middle + first_deviation_backward(grad_normed_one * attention_norm_scale)[0]
    )
    first_norm_portion = select_portion(grad_normed_one)
    first_centered_portion = select_portion(first_centered_scaled)
    gain_terms = lax.psum(
        (
            jnp.sum(first_norm_portion * first_centered_portion, (0, 1)),
            jnp.sum(first_norm_portion, (0, 1)),
            jnp.sum(second_norm_portion * second_centered_portion, (0, 1)),
            jnp.sum(second_norm_portion, (0, 1)),
        ),
        ("dp", "mp"),
    )
    weight_terms = (
        lax.psum(qkv_weight_grad.astype(jnp.bfloat16), "dp").astype(jnp.float32),
        lax.psum(qkv_bias_grad.astype(jnp.bfloat16), "dp").astype(jnp.float32),
        lax.psum(out_weight_grad.astype(jnp.bfloat16), "dp").astype(jnp.float32),
        lax.psum(out_bias_grad.astype(jnp.bfloat16), "dp").astype(jnp.float32),
        lax.psum(in_weight_grad.astype(jnp.bfloat16), "dp").astype(jnp.float32),
        lax.psum(in_bias_grad.astype(jnp.bfloat16), "dp").astype(jnp.float32),
        lax.psum(down_weight_grad.astype(jnp.bfloat16), "dp").astype(jnp.float32),
        lax.psum(down_bias_grad.astype(jnp.bfloat16), "dp").astype(jnp.float32),
    )
    return (
        outputs,
        input_grad,
        gain_terms[0],
        gain_terms[1],
        weight_terms[0],
        weight_terms[1],
        weight_terms[2],
        weight_terms[3],
        gain_terms[2],
        gain_terms[3],
        weight_terms[4],
        weight_terms[5],
        weight_terms[6],
        weight_terms[7],
    )


def solution(mesh):
    return jax.shard_map(
        local,
        mesh=mesh,
        in_specs=(
            P("dp", None, None),
            P("dp", None),
            P(),
            P(),
            P(None, "mp", None),
            P("mp", None),
            P("mp", None, None),
            P(),
            P(),
            P(),
            P(None, "mp"),
            P("mp"),
            P("mp", None),
            P(),
            P("dp", None, None),
        ),
        out_specs=(
            P("dp", "mp", None),
            P("dp", "mp", None),
            P(),
            P(),
            P(None, "mp", None),
            P("mp", None),
            P("mp", None, None),
            P(),
            P(),
            P(),
            P(None, "mp"),
            P("mp"),
            P("mp", None),
            P(),
        ),
        check_vma=False,
    )
```

profile of v0, /device:TPU:0, one launch (start us, length us, event | category | flops | bytes accessed | tf_op | source)
XLA Modules:
  0.0 468.7 jit_solution(11056767459452246908)
XLA Ops:
  11.9 2.8 add_bitcast_fusion
  16.1 21.9 %while.49 = (s32[]{:T(128)}, bf16[2,512,4,64]{1,3,2,0:T(8,128)(2,1)}, f32[2,4,512]{2,1,0:T(4,128)S(1)}, s32[2]{0:T(128)S(1)}, s32[1024]{0:T(1024)S(1)}, /*index=...) while((s32[]{:T(128)}, ...), condition=%wide.region_5.6_spmd.clone, body=%wide.region_2.5_spmd.sunk.clone | while | flops 556267520 | bytes 29173916 | solution.py:70
  22.9 4.1 fusion.143
  33.9 4.1 fusion.143
  42.6 65.5 %all-reduce.16.cloned.1.call-done = f32[1,1024,512]{2,1,0:T(8,128)} async-done(((f32[1,1024,512]{2,1,0:T(8,128)}), f32[1,1024,512]{2,1,0:T(8,128)}) %all-reduce.16.cloned.1.call-update) | async-done | bytes 2097168 | tf_op jit(solution)/shard_map/psum | solution.py:178
  111.0 11.0 %multiply_convert_fusion.1 = (bf16[1024,1024]{1,0:T(8,128)(2,1)}, f32[1024,1024]{1,0:T(8,128)S(1)}, f32[1024,1024]{1,0:T(8,128)S(1)}) fusion(f32[1024]{0:T(1024)S(1)} %copy-done.43, bf16[512,1024]{1,0:T(8,128)(2,1)S(1)} %copy-done, f32[1,1024,512]{2,1,0:T(8,128)S(1)} %subtract_multiply_fusion, f32[512]{0:T(512)S(1)} %copy-done.44, f32[512]{0:T(512)S(1)} %copy-done.37), kind=kOutput, calls=%fused_computation.43 | convolution fusion | flops 1144520704 | bytes 13639680 | tf_op jit(solution)/shard_map/dot_general | solution.py:187
  122.0 3.0 fusion.84
  126.3 2.6 convolution_bitcast_fusion.2
  129.0 4.4 convolution_convert_fusion.1
  135.6 56.3 %all-reduce.18.cloned.1.call-done = f32[1,1024,512]{2,1,0:T(8,128)} async-done(((f32[1,1024,512]{2,1,0:T(8,128)}), f32[1,1024,512]{2,1,0:T(8,128)}) %all-reduce.18.cloned.1.call-update) | async-done | bytes 2097168 | tf_op jit(solution)/shard_map/psum | solution.py:205
  192.0 2.9 multiply_reduce_fusion.1
  199.6 34.7 %while.50 = (s32[]{:T(128)}, f32[1024,4,64]{0,2,1:T(8,128)S(1)}, f32[1024,4,64]{0,2,1:T(8,128)S(1)}, f32[2,512,4,64]{1,3,2,0:T(8,128)}, s32[2]{0:T(128)S(1)}, /*...) while((s32[]{:T(128)}, f32[1024,4,64]{0,2,1:T(8,128)S(1)}, ...), condition=%wide.region_15.16_spmd.clone.clone, body=%wide.region_13.15_spmd.clone.sunk.clone | while | flops 1368913920 | bytes 82905416 | solution.py:111
  204.7 2.4 fusion.155
  207.1 4.1 multiply_reduce_fusion.7
  221.8 2.4 fusion.155
  224.2 4.1 multiply_reduce_fusion.7
  237.4 3.1 mul.507
  245.8 4.2 fusion.52
  252.1 34.2 %all-reduce.8 = (bf16[4,192]{1,0:T(4,128)(2,1)S(1)}, bf16[512]{0:T(512)(128)(2,1)S(1)}, bf16[1024]{0:T(1024)(128)(2,1)S(1)}, bf16[512]{0:T(512)(128)(2,1)S(1)}) all-reduce(bf16[4,192]{1,0:T(4,128)(2,1)S(1)} %get-tuple-element.266, bf16[512]{0:T(512)(128)(2,1)S(1)} %get-tuple-element.264, ...), channel_id=1, replica_groups=mesh['dp'=16,'mp'=2] {'dp'}, use_global_device_ids=true, to_apply=%region_25.26 | all-reduce | flops 2816 | bytes 11264 | tf_op jit(solution)/shard_map/psum | solution.py:246
  290.4 59.8 %all-reduce.20.cloned.1.call-done = (bf16[512,4,192]{0,2,1:T(8,128)(2,1)}, bf16[4,64,512]{2,1,0:T(8,128)(2,1)}, bf16[512,1024]{1,0:T(8,128)(2,1)}, bf16[1024,512]{1,0:T(8,128)(2,1)}) async-done(((bf16[512,4,192]{0,2,1:T(8,128)(2,1)}, bf16[4,64,512]{2,1,0:T(8,128)(2,1)}, bf16[512,1024]{1,0:T(8,128)(2,1)}, bf16[1024,512]{1,0:T(8,128)(2,1)}), (bf16[512,4,192]{0,2,1:T(8,128)(2,1)}, ...) | async-done | bytes 3145744 | tf_op jit(solution)/shard_map/psum | solution.py:245
  352.1 2.5 convert_element_type.139
  354.6 2.8 convert_element_type.145
  359.0 55.9 %all-reduce.22.cloned.1.call-done = (bf16[1,1024,512]{2,1,0:T(8,128)(2,1)}, bf16[1,1024,512]{2,1,0:T(8,128)(2,1)}) async-done(((bf16[1,1024,512]{2,1,0:T(8,128)(2,1)}, bf16[1,1024,512]{2,1,0:T(8,128)(2,1)}), (bf16[1,1024,512]{2,1,0:T(8,128)(2,1)}, bf16[1,1024,512]{2,1,0:T(8,128)(2,1)})) %all-reduce.22.cloned.1.call-update) | async-done | bytes 2097168 | tf_op jit(solution)/shard_map/psum | solution.py:192
  422.4 39.4 %all-reduce.7 = (f32[512]{0:T(512)}, f32[512]{0:T(512)}, f32[512]{0:T(512)}, f32[512]{0:T(512)}) all-reduce(f32[512]{0:T(512)S(1)} %get-tuple-element.211, f32[512]{0:T(512)S(1)} %get-tuple-element.210, f32[512]{0:T(512)S(1)} %get-tuple-element.209, f32[512]{0:T(512)S(1)} %get-tuple-element.208), channel_id=1, replica_groups=mesh['dp'=16,'mp'=2] {'dp','mp'}, use_global_device_ids=true, to_apply=%region_20.21 | all-reduce | flops 2048 | bytes 16384 | tf_op jit(solution)/shard_map/psum | solution.py:235
  (193 shorter events, 72.7 us)
Async XLA Ops:
  7.2 103.8 %copy-start = (bf16[512,1024]{1,0:T(8,128)(2,1)S(1)}, bf16[512,1024]{1,0:T(8,128)(2,1)}, u32[]{:S(2)}) copy-start(bf16[512,1024]{1,0:T(8,128)(2,1)} %param.29) | copy-start | bytes 3145732
  7.2 101.0 %all-reduce.16.cloned.1.call-start = ((), (), s32[]{:S(2)}) async-start(), calls=%async_computation | async-start | bytes 4194304 | tf_op jit(solution)/shard_map/psum | solution.py:178
  9.6 5.1 %copy-start.31 = (f32[1024]{0:T(1024)}, f32[1024]{0:T(1024)S(1)}, u32[]{:S(2)}) copy-start(f32[1024]{0:T(1024)S(1)} %broadcast_multiply_fusion.2) | copy-start | bytes 12292
  11.8 3.7 copy-start.19
  16.0 24.5 %copy-start.28 = (bf16[4,64,512]{2,1,0:T(8,128)(2,1)S(1)}, bf16[4,64,512]{2,1,0:T(8,128)(2,1)}, u32[]{:S(2)}) copy-start(bf16[4,64,512]{2,1,0:T(8,128)(2,1)} %param.25) | copy-start | bytes 786436
  38.0 70.2 %copy-start.5 = (bf16[1,1024,512]{2,1,0:T(8,128)(2,1)S(1)}, bf16[1,1024,512]{2,1,0:T(8,128)(2,1)}, u32[]{:S(2)}) copy-start(bf16[1,1024,512]{2,1,0:T(8,128)(2,1)} %param.19) | copy-start | bytes 3145732
  38.0 70.2 %copy-start.39 = (f32[512]{0:T(512)S(1)}, f32[512]{0:T(512)}, u32[]{:S(2)}) copy-start(f32[512]{0:T(512)} %param.26) | copy-start | bytes 6148
  42.4 149.6 %all-reduce.18.cloned.1.call-start = ((), (), s32[]{:S(2)}) async-start(), calls=%async_computation.1 | async-start | bytes 4194304 | tf_op jit(solution)/shard_map/psum | solution.py:205
  110.1 11.9 %copy-start.2 = (f32[1,1024,512]{2,1,0:T(8,128)}, f32[1,1024,512]{2,1,0:T(8,128)S(1)}, u32[]{:S(2)}) copy-start(f32[1,1024,512]{2,1,0:T(8,128)S(1)} %get-tuple-element.275) | copy-start | bytes 6291460
  111.0 11.0 %copy-start.13 = (f32[1,1024,512]{2,1,0:T(8,128)}, f32[1,1024,512]{2,1,0:T(8,128)S(1)}, u32[]{:S(2)}) copy-start(f32[1,1024,512]{2,1,0:T(8,128)S(1)} %subtract_multiply_fusion) | copy-start | bytes 6291460
  111.0 11.0 %copy-start.26 = (bf16[1,1024,512]{2,1,0:T(8,128)(2,1)S(1)}, bf16[1,1024,512]{2,1,0:T(8,128)(2,1)}, u32[]{:S(2)}) copy-start(bf16[1,1024,512]{2,1,0:T(8,128)(2,1)} %param.33) | copy-start | bytes 3145732
  111.0 11.0 %copy-start.41 = (bf16[1024,512]{1,0:T(8,128)(2,1)S(1)}, bf16[1024,512]{1,0:T(8,128)(2,1)}, u32[]{:S(2)}) copy-start(bf16[1024,512]{1,0:T(8,128)(2,1)} %param.31) | copy-start | bytes 3145732
  128.9 221.3 %all-reduce.20.cloned.1.call-start = ((), (), s32[]{:S(2)}) async-start(), calls=%async_computation.2 | async-start | bytes 6291456 | tf_op jit(solution)/shard_map/psum | solution.py:245
  129.0 4.4 copy-start.14
  129.0 4.4 copy-start.47
  234.3 6.3 %copy-start.20 = (f32[1024,32]{0,1:T(8,128)S(1)}, f32[1024,32]{0,1:T(8,128)}, u32[]{:S(2)}) copy-start(f32[1024,32]{0,1:T(8,128)} %copy-done.19) | copy-start | bytes 393220
  234.3 6.3 %copy-start.22 = (f32[1024,32]{0,1:T(8,128)S(1)}, f32[1024,32]{0,1:T(8,128)}, u32[]{:S(2)}) copy-start(f32[1024,32]{0,1:T(8,128)} %copy-done.21) | copy-start | bytes 393220
  245.8 4.3 copy-start.18
  245.8 169.1 %all-reduce.22.cloned.1.call-start = ((), (), s32[]{:S(2)}) async-start(), calls=%async_computation.3 | async-start | bytes 4194304 | tf_op jit(solution)/shard_map/psum | solution.py:192
  245.8 4.2 copy-start.42
  350.2 7.2 %copy-start.23 = (bf16[1024,512]{1,0:T(8,128)(2,1)S(1)}, bf16[1024,512]{1,0:T(8,128)(2,1)}, u32[]{:S(2)}) copy-start(bf16[1024,512]{1,0:T(8,128)(2,1)} %get-tuple-element.261) | copy-start | bytes 3145732
  357.4 60.9 %copy-start.34 = (f32[1024]{0:T(1024)S(1)}, f32[1024]{0:T(1024)}, u32[]{:S(2)}) copy-start(f32[1024]{0:T(1024)} %copy-done.33) | copy-start | bytes 12292
  357.4 60.9 %copy-start.7 = (bf16[1,1024,512]{2,1,0:T(8,128)(2,1)S(1)}, bf16[1,1024,512]{2,1,0:T(8,128)(2,1)}, u32[]{:S(2)}) copy-start(bf16[1,1024,512]{2,1,0:T(8,128)(2,1)} %param.19) | copy-start | bytes 3145732
  418.4 43.4 %copy-start.1 = (bf16[512,1024]{1,0:T(8,128)(2,1)S(1)}, bf16[512,1024]{1,0:T(8,128)(2,1)}, u32[]{:S(2)}) copy-start(bf16[512,1024]{1,0:T(8,128)(2,1)} %param.29) | copy-start | bytes 3145732
  (31 other events, 56.7 us)
Sparse Core Ops, SparseCore 0:
  42.5 65.5 all-reduce.15
  129.0 62.8 all-reduce.17
  245.9 104.2 all-reduce.19
  353.0 61.8 all-reduce.21
where the time goes:
time: 476 us; the launch traced here: 469 us
  waiting for transfers between devices  238 us (50%)
  blocking collectives  73.6 us (15%)
  matrix products  70.4 us (15%)
  other arithmetic  44.7 us (9%)
  local copies, waits for them, and re-layouts  17.5 us (4%)
  between operations  14.9 us (3%)
  loops' own time  9.69 us (2%)
    psum x1, waiting for transfers between devices, local(): attn_summed = lax.psum(attn_part, 'mp')  65.5 us
    psum x1, waiting for transfers between devices, local(): lax.psum(qkv_weight_grad.astype(jnp.bfloat16), 'dp').astype(jnp.float32)  59.8 us
    psum x1, waiting for transfers between devices, local(): grad_normed_two = lax.psum(norm_two_part, 'mp')  56.3 us
    psum x1, waiting for transfers between devices, local(): lax.psum(ffn_part.astype(jnp.bfloat16), 'mp').astype(jnp.float32)  55.9 us
    psum x1, blocking collectives, local(): lax.psum((jnp.sum(first_norm_portion * first_centered_portion, (0, 1)), j...  39.4 us
    psum x1, blocking collectives, local(): lax.psum(qkv_bias_grad.astype(jnp.bfloat16), 'dp').astype(jnp.float32)  34.2 us
    dot_general x1, matrix products, local(): jnp.dot(flat_two, in_weight, preferred_element_type=jnp.float32) + in_bias  11 us
    dot_general x4, matrix products, contract_rows(): lax.dot_general(left, right, (((0,), (0,)), ((), ())), preferred_element_...  9.78 us
  transfers between devices with their start and end apart: 4, of which 4 were waited for; matrix products, arithmetic and copies ran while one was open for 5% of the time, Pallas kernels for 0%

commit v1 on v0

--- a/solution.py
+++ b/solution.py
@@ -1,12 +1,562 @@
+import functools
 import math
 
 import jax
 import jax.numpy as jnp
+import numpy as np
 from jax import lax
+from jax.experimental import pallas as pl
+from jax.experimental.pallas import tpu as pltpu
 from jax.sharding import PartitionSpec as P
 
-EPS = 1e-05
-NEG = -1e30
+f32, bf = jnp.float32, jnp.bfloat16
+EPS = 1e-5
+BIG = 1e30
+LOG2E = math.log2(math.e)
+AUG = 16
+ERFCX_P = 0.425
+ERFCX = (
+    0.23971980880709728, 0.24117083247455387, 0.20509840538640725, 0.239985627333635,
+    -0.07373126048981057, 0.3746498195367672, -0.29358684214803077, 0.06669325662319364,
+)
+MESH = pl.DeviceIdType.MESH
+CHUNKS = ((0, 1024), (1024, 1024), (2048, 256), (2304, 768))
+MODES = ("yx", "yx", "yx", "yx")
+ROWS_SIDE = 3072
+
+
+def dg(a, b, ca, cb):
+    return lax.dot_general(a, b, (((ca,), (cb,)), ((), ())), preferred_element_type=f32)
+
+
+def gelu_parts(u):
+    ex = jnp.exp2(u * u * (-0.5 * LOG2E))
+    t = 1.0 / (1.0 + (ERFCX_P / math.sqrt(2.0)) * jnp.abs(u))
+    poly = 0.5 * ERFCX[-1]
+    for c in ERFCX[-2::-1]:
+        poly = poly * t + 0.5 * c
+    tail = poly * t * ex
+    phi_cum = jnp.where(u >= 0, 1.0 - tail, tail)
+    return u * phi_cum, phi_cum + u * ex * (1.0 / math.sqrt(2 * math.pi))
+
+
+def norm_rows(x):
+    c = x - jnp.mean(x, -1, keepdims=True)
+    rs = lax.rsqrt(jnp.mean(c * c, -1, keepdims=True) + EPS)
+    return c * rs, rs
+
+
+class Comm:
+    def __init__(self, ssem, rsem):
+        d, self.y = lax.axis_index("dp"), lax.axis_index("mp")
+        self.z, self.x, self.c = d // 4, (d // 2) % 2, d % 2
+        self.ssem, self.rsem, self.n, self.started = ssem, rsem, 0, []
+
+    def dev(self, z=None, x=None, y=None, c=None):
+        z, x, y, c = (b if a is None else a for a, b in ((z, self.z), (x, self.x), (y, self.y), (c, self.c)))
+        return ((z * 2 + x) * 2 + c, y)
+
+    def core(self):
+        return self.dev(c=1 - self.c)
+
+    def yy(self):
+        return self.dev(y=1 - self.y)
+
+    def xx(self):
+        return self.dev(x=1 - self.x)
+
+    def zz(self, k):
+        return self.dev(z=lax.rem(self.z + k, 4))
+
+    def partners(self):
+        return [self.core(), self.yy(), self.xx()] + [self.zz(k) for k in (1, 2, 3)]
+
+    def copy(self, src, dst, target):
+        i = self.n
+        self.n += 1
+
+        def make():
+            return pltpu.make_async_remote_copy(
+                src_ref=src, dst_ref=dst, send_sem=self.ssem.at[i], recv_sem=self.rsem.at[i],
+                device_id=target, device_id_type=MESH)
+        self.started.append(make)
+        return make
+
+    def drain(self):
+        for make in self.started:
+            make().wait_send()
+
+
+def rows(start, size):
+    return pl.ds(pl.multiple_of(start, 16), size)
+
+
+def mega(x_h, seg_ref, g1_ref, b1_ref, wt_h, qb_ref, ow_h, ob_ref, g2_ref, b2_ref, iw_h, ib_ref, dw_h, db_ref, ct_h, cos_h, sin_h,
+         out_ref, ig_ref, fin_ref, vout_ref,
+         x_v, ct_v, cos_v, sin_v, wt, ow, iw, dw, qb, ib,
+         normed, normed_t, kq, kk, kv, e_ref, att, attb, rr, dob, ds, gp, normed2, normed2t, xh2, acc_o, acc_g, gm,
+         grad, cr, yr, xr, zr, gn_own, gn_oth, gn_in, vec, vcr, vyr, vxr, vzr,
+         lsem, ssem, rsem):
+    A, D = x_v.shape
+    T = ct_v.shape[0]
+    H = 8
+    HD = 64
+    RB = 256
+    QB = 256
+    cm = Comm(ssem, rsem)
+    own0 = pl.multiple_of(cm.y * T, T)
+    oth0 = pl.multiple_of((1 - cm.y) * T, T)
+    starts = (own0, oth0)
+
+    barrier = pltpu.get_barrier_semaphore()
+    for t in cm.partners():
+        pl.semaphore_signal(barrier, inc=1, device_id=t, device_id_type=MESH)
+
+    loads = [
+        (x_h.at[pl.ds(own0, T)], x_v.at[pl.ds(0, T)]), (x_h.at[pl.ds(oth0, T)], x_v.at[pl.ds(T, T)]),
+        (wt_h, wt.at[0]), (cos_h.at[:, pl.ds(own0, T)], cos_v.at[0]), (cos_h.at[:, pl.ds(oth0, T)], cos_v.at[1]),
+        (sin_h.at[:, pl.ds(own0, T)], sin_v.at[0]), (sin_h.at[:, pl.ds(oth0, T)], sin_v.at[1]),
+        (ow_h, ow.at[0]), (ct_h.at[pl.ds(own0, T)], ct_v), (iw_h, iw.at[0]), (dw_h, dw.at[0]),
+    ]
+    loads = [pltpu.make_async_copy(s, d, lsem.at[i]) for i, (s, d) in enumerate(loads)]
+    for c in loads:
+        c.start()
+    qb[0:4, :] = qb_ref[...]
+    ib[0:1, :] = ib_ref[...]
+
+    quarter = cm.c * 2 + cm.x
+    qother = cm.c * 2 + (1 - cm.x)
+    parts = []
+
+    def piece(src, dst, cols, r0, total, subs):
+        q = total // 4
+        n = q // subs
+        item = {"y": [], "x": []}
+        for s in range(subs):
+            a = rows(r0 + quarter * q + s * n, n)
+            item["y"].append(cm.copy(src.at[a, cols], dst.at[a, cols], cm.yy()))
+            item["x"].append(cm.copy(dst.at[a, cols], dst.at[a, cols], cm.xx()))
+        h = rows(r0 + cm.c * (total // 2), total // 2)
+        item["c"] = [cm.copy(dst.at[h, cols], dst.at[h, cols], cm.core())]
+        return item
+
+    full = pl.ds(0, D)
+    g_wt = piece(wt_h, wt.at[1], full, 0, 768, 2)
+    g_ow = piece(ow_h, ow.at[1], full, 0, 256, 1)
+    g_iw = [piece(iw_h, iw.at[1], pl.ds(j * 512, 512), 0, 512, 1) for j in range(2)]
+    g_dw = [piece(dw_h, dw.at[1], full, j * 512, 512, 1) for j in range(2)]
+    g_qb = cm.copy(qb_ref, qb.at[pl.ds(8, 4)], cm.yy())
+    g_ib = cm.copy(ib_ref, ib.at[pl.ds(8, 1)], cm.yy())
+    gathers = [g_wt, g_ow, g_iw[0], g_dw[0], g_iw[1], g_dw[1]]
+
+    def start_gather():
+        for it in gathers:
+            for mk in it["y"]:
+                mk().start()
+            if it is g_wt:
+                g_qb().start()
+                g_ib().start()
+
+    def fwd_x(it, s=None):
+        for i, (my, mx) in enumerate(zip(it["y"], it["x"])):
+            if s is None or s == i:
+                my().wait_recv()
+                mx().start()
+
+    def fwd_c(it):
+        for mx in it["x"]:
+            mx().wait_recv()
+        it["c"][0]().start()
+
+    def ready(it):
+        it["c"][0]().wait_recv()
+
+    def chunk_stages(k):
+        r0, R = CHUNKS[k]
+        h, q, p = R // 2, R // 4, R // 16
+        own, oth = grad.at[0], grad.at[1]
+        lo = r0 + cm.c * h
+        keep = rows(lo, h)
+        give = rows(r0 + (1 - cm.c) * h, h)
+        slot = rows(r0 // 2, h)
+        qx, qo = lo + cm.x * q, lo + (1 - cm.x) * q
+        px = qx + cm.z * p
+        st = {}
+        core_oth = cm.copy(oth.at[give], cr.at[1, slot], cm.core())
+        core_own = cm.copy(own.at[give], cr.at[0, slot], cm.core())
+        zs = [cm.copy(own.at[rows(qx + lax.rem(cm.z + j, 4) * p, p)], zr.at[j - 1, rows(r0 // 16, p)], cm.zz(j)) for j in (1, 2, 3)]
+        agz = [cm.copy(fin_ref.at[rows(px, p)], fin_ref.at[rows(px, p)], cm.zz(j)) for j in (1, 2, 3)]
+        agx = cm.copy(fin_ref.at[rows(qx, q)], fin_ref.at[rows(qx, q)], cm.xx())
+        agc = cm.copy(fin_ref.at[keep], fin_ref.at[keep], cm.core())
+        st["oth"] = lambda: core_oth().start()
+        st["own"] = lambda: core_own().start()
+        ycp = cm.copy(oth.at[keep], yr.at[slot], cm.yy())
+        xslot = rows(r0 // 4, q)
+        xcp = cm.copy(own.at[rows(qo, q)], xr.at[xslot], cm.xx())
+
+        def s_y():
+            core_oth().wait_recv()
+            oth[keep] = (oth[keep].astype(f32) + cr[1, slot].astype(f32)).astype(bf)
+            ycp().start()
+
+        def s_x():
+            core_own().wait_recv()
+            ycp().wait_recv()
+            own[keep] = (own[keep].astype(f32) + cr[0, slot].astype(f32) + yr[slot].astype(f32)).astype(bf)
+            xcp().start()
+
+        def s_z():
+            xcp().wait_recv()
+            qq = rows(qx, q)
+            own[qq] = (own[qq].astype(f32) + xr[xslot].astype(f32)).astype(bf)
+            for c in zs:
+                c().start()
+
+        def s_agz():
+            acc = own[rows(px, p)].astype(f32)
+            for j, c in enumerate(zs):
+                c().wait_recv()
+                acc = acc + zr[j, rows(r0 // 16, p)].astype(f32)
+            fin_ref[rows(px, p)] = acc.astype(bf)
+            for c in agz:
+                c().start()
+
+        def s_agx():
+            for c in agz:
+                c().wait_recv()
+            agx().start()
+
+        def s_agc():
+            agx().wait_recv()
+            agc().start()
+
+        def s_end():
+            agc().wait_recv()
+
+        st.update(y=s_y, x=s_x, z=s_z, agz=s_agz, agx=s_agx, agc=s_agc, end=s_end)
+        return st
+
+    red = [chunk_stages(k) for k in range(4)]
+    gn_cp = cm.copy(gn_oth, gn_in, cm.yy())
+    v_core = cm.copy(vec, vcr, cm.core())
+    v_y = cm.copy(vec.at[1], vyr, cm.yy())
+    v_x = cm.copy(vec.at[0], vxr, cm.xx())
+    v_z = [cm.copy(vzr.at[cm.z], vzr.at[cm.z], cm.zz(j)) for j in (1, 2, 3)]
+
+    def norm1(i):
+        loads[i].wait()
+        for r in range(0, T, RB):
+            xh, _ = norm_rows(x_v[pl.ds(i * T + r, RB), :].astype(f32))
+            normed[pl.ds(i * T + r, RB), :] = (xh * g1_ref[...] + b1_ref[...]).astype(bf)
+        normed_t[:, i * T:(i + 1) * T] = normed[i * T:(i + 1) * T, :].T
+
+    norm1(0)
+    pl.semaphore_wait(barrier, 6)
+    start_gather()
+    norm1(1)
+
+    row = lax.broadcasted_iota(jnp.int32, (AUG, T), 0)
+    so = seg_ref[:, pl.ds(own0, T)]
+    sth = seg_ref[:, pl.ds(oth0, T)]
+    q_aug = jnp.where(row == so, 1.0, 0.0).astype(bf)
+    k_aug = [jnp.where((row == s) | (row >= 4), 0.0, -BIG).astype(bf) for s in (so, sth)]
+    v_aug = jnp.where(row < 2, 1.0, 0.0).astype(bf)
+    for i in range(2, 7):
+        loads[i].wait()
+
+    fwd_hooks = {
+        2: [lambda: fwd_x(g_wt)],
+        4: [lambda: fwd_c(g_wt), lambda: fwd_x(g_ow), lambda: g_qb().wait_recv(), lambda: ready(g_wt)],
+        5: [lambda: fwd_x(g_iw[0]), lambda: fwd_c(g_ow)],
+        6: [lambda: fwd_x(g_dw[0])],
+        7: [lambda: fwd_c(g_iw[0]), lambda: fwd_x(g_iw[1])],
+    }
+
+    def run_hooks(hooks, h):
+        for k, fs in hooks.items():
+            @pl.when(h == k)
+            def _():
+                for f in fs:
+                    f()
+
+    def head_fwd(h, carry):
+        run_hooks(fwd_hooks, h)
+        side, hh = h // 4, lax.rem(h, 4)
+        w = wt[side, pl.ds(pl.multiple_of(hh * 192, 64), 192), :]
+        bcol = jnp.broadcast_to(qb[pl.ds(side * 8 + hh, 1), :], (128, 192)).T
+        bcol = jnp.concatenate([bcol] * (T // 128), axis=1)
+        for i in range(2):
+            cos, sin = cos_v[i], sin_v[i]
+            lo = 0 if i == 0 else 64
+            p = dg(w[lo:], normed_t[:, i * T:(i + 1) * T], 1, 0) + bcol[lo:]
+            if i == 0:
+                a, b = p[0:32], p[32:64]
+                sc = LOG2E / math.sqrt(HD)
+                kq[h, 0:32, :] = ((a * cos - b * sin) * sc).astype(bf)
+                kq[h, 32:64, :] = ((b * cos + a * sin) * sc).astype(bf)
+                kq[h, 64:, :] = q_aug
+                p = p[64:]
+            sl = slice(i * T, (i + 1) * T)
+            a, b = p[0:32], p[32:64]
+            kk[h, 0:32, sl] = (a * cos - b * sin).astype(bf)
+            kk[h, 32:64, sl] = (b * cos + a * sin).astype(bf)
+            kk[h, 64:, sl] = k_aug[i]
+            kv[h, 0:64, sl] = p[64:].astype(bf)
+            kv[h, 64:, sl] = v_aug
+        for q0 in range(0, T, QB):
+            s = dg(kk[h], kq[h, :, q0:q0 + QB], 0, 0)
+            mx = jnp.max(s, axis=0, keepdims=True)
+            e = jnp.exp2(s - mx).astype(bf)
+            e_ref[h, :, q0:q0 + QB] = e
+            o = dg(kv[h], e, 1, 0)
+            r = 1.0 / o[64:65]
+            rr[pl.ds(h, 1), q0:q0 + QB] = r
+            o = o[:64] * r
+            hs = pl.ds(pl.multiple_of(h * 64, 64), 64)
+            att[hs, q0:q0 + QB] = o
+            attb[hs, q0:q0 + QB] = o.astype(bf)
+        return carry
+
+    lax.fori_loop(0, H, head_fwd, 0)
+
+    for i in (7, 8):
+        loads[i].wait()
+    ready(g_ow)
+    fwd_c(g_dw[0])
+    fwd_x(g_dw[1])
+    mid = x_v[0:T, :].astype(f32) + ob_ref[...]
+    for s in range(2):
+        mid = mid + dg(attb[s * 256:(s + 1) * 256, :], ow[s], 0, 0)
+    acc_o[...] = mid
+    rs2 = []
+    for r in range(0, T, RB):
+        xh, rs = norm_rows(acc_o[r:r + RB, :])
+        rs2.append(rs)
+        xh2[r:r + RB, :] = xh
+        normed2[r:r + RB, :] = (xh * g2_ref[...] + b2_ref[...]).astype(bf)
+    normed2t[...] = normed2[...].T
+    acc_o[...] += db_ref[...]
+    acc_g[...] = jnp.zeros_like(acc_g)
+    for i in (9, 10):
+        loads[i].wait()
+    ready(g_iw[0])
+    ready(g_dw[0])
+    g_ib().wait_recv()
+
+    ffn_hooks = {
+        1: [red[0]["oth"], lambda: fwd_c(g_iw[1]), lambda: fwd_c(g_dw[1])],
+        2: [red[0]["own"], red[0]["y"], lambda: ready(g_iw[1]), lambda: ready(g_dw[1])],
+        3: [red[1]["oth"]],
+    }
+
+    def ffn(f, carry):
+        run_hooks(ffn_hooks, f)
+        side, j = 1 - lax.rem(f, 2), f // 2
+        cols = pl.ds(pl.multiple_of(j * 512, 512), 512)
+        w, d = iw[side, :, cols], dw[side, cols, :]
+        u = dg(normed2[...], w, 1, 0) + ib[pl.ds(side * 8, 1), cols]
+        act, dge = gelu_parts(u)
+        act = act.astype(bf)
+        acc_o[...] += dg(act, d, 1, 0)
+        ga = dg(ct_v[...], d, 1, 1)
+        gh = (ga * dge).astype(bf)
+        acc_g[...] += dg(gh, w, 1, 1)
+        r0 = pl.multiple_of(j * 1024, 1024)
+        grad[side, pl.ds(r0, 512), :] = dg(normed2t[...], gh, 1, 0).astype(bf)
+        grad[side, pl.ds(r0 + 512, 512), :] = dg(act, ct_v[...], 0, 0).astype(bf)
+        vec[side, pl.ds(6 + j, 1), :] = jnp.sum(gh.astype(f32), 0, keepdims=True)
+        return carry
+
+    lax.fori_loop(0, 4, ffn, 0)
+    red[1]["own"]()
+    out_ref[...] = acc_o[...]
+
+    vec[:, 12:16, :] = jnp.zeros((2, 4, 512), f32)
+    vec[:, 8:12, :] = jnp.zeros((2, 4, 512), f32)
+    for r in range(0, T, RB):
+        gn = acc_g[r:r + RB, :]
+        xh = xh2[r:r + RB, :]
+        v = [jnp.sum(gn * xh, 0, keepdims=True), jnp.sum(gn, 0, keepdims=True)]
+        h = gn * g2_ref[...]
+        ct = ct_v[r:r + RB, :].astype(f32)
+        g = ct + rs2[r // RB] * (h - jnp.mean(h, -1, keepdims=True) - xh * jnp.mean(h * xh, -1, keepdims=True))
+        gm[r:r + RB, :] = g
+        gb = g.astype(bf)
+        normed2[r:r + RB, :] = gb
+        v += [jnp.sum(gb.astype(f32), 0, keepdims=True), jnp.sum(ct, 0, keepdims=True)]
+        for i, a in enumerate(v):
+            a = a if r == 0 else vec[0, i:i + 1, :] + a
+            vec[0, i:i + 1, :] = a
+            vec[1, i:i + 1, :] = a
+    red[1]["y"]()
+    gb = normed2[...]
+    for s in range(2):
+        grad[s, 2048:2304, :] = dg(attb[s * 256:(s + 1) * 256, :], gb, 1, 0).astype(bf)
+    red[2]["oth"]()
+    red[2]["own"]()
+    for s in range(2):
+        acc_o[s * 256:(s + 1) * 256, :] = dg(ow[s], gb, 1, 1)
+
+    row2 = lax.broadcasted_iota(jnp.int32, (AUG, T), 0)
+    bwd_hooks = {
+        1: [red[2]["y"]],
+        4: [red[0]["x"]],
+        6: [red[0]["z"]],
+        7: [red[0]["agz"]],
+    }
+
+    def head_bwd(h, carry):
+        run_hooks(bwd_hooks, h)
+        hs = pl.ds(pl.multiple_of(h * 64, 64), 64)
+        d = (acc_o[hs, :] * rr[pl.ds(h, 1), :]).astype(bf)
+        dob[:64, :] = d
+        dl = jnp.sum(d.astype(f32) * att[hs, :], 0, keepdims=True)
+        hi = dl.astype(bf).astype(f32)
+        dob[64:, :] = jnp.where(row2 == 0, -hi, jnp.where(row2 == 1, hi - dl, 0.0)).astype(bf)
+        for q0 in range(0, T, QB):
+            dp = dg(kv[h], dob[:, q0:q0 + QB], 0, 0)
+            ds[:, q0:q0 + QB] = (dp * e_ref[h, :, q0:q0 + QB].astype(f32)).astype(bf)
+        dq = dg(kk[h, :64, :], ds[...], 1, 0) * (1.0 / math.sqrt(HD))
+        dk = dg(kq[h, :64, :], ds[...], 1, 1) * (1.0 / LOG2E)
+        dv = dg(dob[:64, :], e_ref[h], 1, 1)
+        b0 = pl.multiple_of(h * 192, 64)
+        a, b = dq[:32], dq[32:]
+        gp[pl.ds(b0, 32), :T] = (a * cos_v[0] + b * sin_v[0]).astype(bf)
+        gp[pl.ds(b0 + 32, 32), :T] = (b * cos_v[0] - a * sin_v[0]).astype(bf)
+        gp[pl.ds(b0, 64), T:] = jnp.zeros((64, A - T), bf)
+        for i in range(2):
+            sl = slice(i * T, (i + 1) * T)
+            a, b = dk[:32, sl], dk[32:, sl]
+            gp[pl.ds(b0 + 64, 32), sl] = (a * cos_v[i] + b * sin_v[i]).astype(bf)
+            gp[pl.ds(b0 + 96, 32), sl] = (b * cos_v[i] - a * sin_v[i]).astype(bf)
+        gp[pl.ds(b0 + 128, 64), :] = dv.astype(bf)
+        return carry
+
+    lax.fori_loop(0, H, head_bwd, 0)
+    red[0]["agx"]()
+    for s in (1, 0):
+        grad[s, 2304:3072, :] = dg(gp[s * 768:(s + 1) * 768, :], normed[...], 1, 0).astype(bf)
+        red[3]["oth" if s else "own"]()
+    red[1]["x"]()
+    red[3]["y"]()
+    gn_oth[...] = (dg(gp[:768, T:], wt[0], 0, 0) + dg(gp[768:, T:], wt[1], 0, 0)).astype(bf)
+    gn_cp().start()
+    red[0]["agc"]()
+    red[1]["z"]()
+    qg = dg(jnp.ones((AUG, A), bf), gp[...], 1, 1)
+    for h in range(H):
+        vec[h // 4, 8 + h % 4:9 + h % 4, 0:192] = qg[0:1, h * 192:(h + 1) * 192]
+    gn_own[...] = dg(gp[:768, :T], wt[0], 0, 0) + dg(gp[768:, :T], wt[1], 0, 0)
+    for i, ref in enumerate((gn_own, gn_oth)):
+        for r in range(0, T, RB):
+            xh, _ = norm_rows(x_v[pl.ds(i * T + r, RB), :].astype(f32))
+            gn = ref[r:r + RB, :].astype(f32)
+            for j, a in enumerate((jnp.sum(gn * xh, 0, keepdims=True), jnp.sum(gn, 0, keepdims=True))):
+                a = a if (r == 0 and i == 0) else vec[0, 4 + j:5 + j, :] + a
+                vec[0, 4 + j:5 + j, :] = a
+                vec[1, 4 + j:5 + j, :] = a
+    v_core().start()
+    red[1]["agz"]()
+    red[2]["x"]()
+    v_core().wait_recv()
+    v_core().wait_send()
+    vec[...] += vcr[...]
+    v_y().start()
+    red[2]["z"]()
+    red[1]["agx"]()
+    red[3]["x"]()
+    red[2]["agz"]()
+    red[1]["agc"]()
+    red[3]["z"]()
+    red[2]["agx"]()
+    v_y().wait_recv()
+    vec[0] = vec[0] + vyr[...]
+    v_x().start()
+    red[3]["agz"]()
+    red[2]["agc"]()
+    v_x().wait_recv()
+    vzr[cm.z] = vec[0] + vxr[...]
+    for c in v_z:
+        c().start()
+    red[3]["agx"]()
+    gn_cp().wait_recv()
+    for r in range(0, T, RB):
+        xh, rs = norm_rows(x_v[r:r + RB, :].astype(f32))
+        h = (gn_own[r:r + RB, :] + gn_in[r:r + RB, :].astype(f32)) * g1_ref[...]
+        ig_ref[r:r + RB, :] = gm[r:r + RB, :] + rs * (h - jnp.mean(h, -1, keepdims=True) - xh * jnp.mean(h * xh, -1, keepdims=True))
+    red[3]["agc"]()
+    for c in v_z:
+        c().wait_recv()
+    vout_ref[...] = (vzr[0] + vzr[1]) + (vzr[2] + vzr[3])
+    for k in range(4):
+        red[k]["end"]()
+    skip = cm.started.index(v_core)
+    for i, make in enumerate(cm.started):
+        if i != skip:
+            make().wait_send()
+
+
+N_SEM = 96
+
+
+def call_mega(x, seg, g1, b1, wt, qb, ow, ob, g2, b2, iw, ib, dw, db, ct, cos, sin):
+    A, D = x.shape
+    T, R = A // 2, 768
+    V = pl.BlockSpec(memory_space=pltpu.VMEM)
+    N = pl.BlockSpec(memory_space=pl.ANY)
+    S = jax.ShapeDtypeStruct
+    outs = [S((T, D), f32), S((T, D), f32), S((ROWS_SIDE, D), bf), S((16, D), f32)]
+    K = 64 + AUG
+    shapes = [
+        ((A, D), bf), ((T, D), bf), ((2, 32, T), f32), ((2, 32, T), f32), ((2, R, D), bf), ((2, 256, D), bf), ((2, D, 1024), bf), ((2, 1024, D), bf), ((16, 192), f32), ((16, 1024), f32),
+        ((A, D), bf), ((D, A), bf), ((8, K, T), bf), ((8, K, A), bf), ((8, K, A), bf), ((8, A, T), bf), ((512, T), f32), ((512, T), bf), ((8, T), f32), ((K, T), bf), ((A, T), bf), ((2 * R, A), bf), ((T, D), bf), ((D, T), bf), ((T, D), f32), ((T, D), f32), ((T, D), f32), ((T, D), f32),
+        ((2, ROWS_SIDE, D), bf), ((2, ROWS_SIDE // 2, D), bf), ((ROWS_SIDE // 2, D), bf), ((ROWS_SIDE // 4, D), bf), ((3, ROWS_SIDE // 16, D), bf), ((T, D), f32), ((T, D), bf), ((T, D), bf),
+        ((2, 16, D), f32), ((2, 16, D), f32), ((16, D), f32), ((16, D), f32), ((4, 16, D), f32),
+    ]
+    scratch = [pltpu.VMEM(s, d) for s, d in shapes] + [pltpu.SemaphoreType.DMA((11,)), pltpu.SemaphoreType.DMA((N_SEM,)), pltpu.SemaphoreType.DMA((N_SEM,))]
+    return pl.pallas_call(
+        mega, out_shape=outs,
+        in_specs=[N, V, V, V, N, V, N, V, V, V, N, V, N, V, N, N, N], out_specs=[V] * 4, scratch_shapes=scratch,
+        compiler_params=pltpu.CompilerParams(vmem_limit_bytes=62 * 2**20, collective_id=0, has_side_effects=True),
+    )(x, seg, g1, b1, wt, qb, ow, ob, g2, b2, iw, ib, dw, db, ct, cos, sin)
+
+
+def finish(fin, vec, qkv, ow, iw, dw, qb, ib, *small):
+    for j in range(2):
+        iw[:, j * 512:(j + 1) * 512] = fin[j * 1024:j * 1024 + 512, :].astype(f32)
+        dw[j * 512:(j + 1) * 512, :] = fin[j * 1024 + 512:(j + 1) * 1024, :].astype(f32)
+        ib[:, j * 512:(j + 1) * 512] = vec[6 + j:7 + j, :]
+    ow[...] = fin[2048:2304, :].astype(f32)
+    qkv[...] = fin[2304:3072, :].astype(f32)
+    qb[...] = vec[8:12, 0:192]
+    for i, ref in enumerate(small):
+        ref[...] = vec[i:i + 1, :]
+
+
+def call_finish(fin, vec):
+    D = fin.shape[1]
+    V = pl.BlockSpec(memory_space=pltpu.VMEM)
+    S = jax.ShapeDtypeStruct
+    outs = [S(s, f32) for s in ((768, D), (256, D), (D, 1024), (1024, D), (4, 192), (1, 1024)) + ((1, D),) * 6]
+    return pl.pallas_call(finish, out_shape=outs, in_specs=[V, V], out_specs=[V] * len(outs),
+                          compiler_params=pltpu.CompilerParams(vmem_limit_bytes=40 * 2**20))(fin, vec)
+
+
+def tables(length, half):
+    fr = np.exp(np.arange(half, dtype=np.float64) * (-math.log(10000.0) / half))
+    an = fr[:, None] * np.arange(length)[None, :]
+    return np.cos(an).astype(np.float32), np.sin(an).astype(np.float32)
+
+
+def local(inputs, seg, g1, b1, qkv_w, qkv_b, out_w, out_b, g2, b2, in_w, in_b, down_w, down_b, cot):
+    A, D = inputs.shape[1:]
+    cos, sin = tables(A, 32)
+    r1 = lambda v: v.reshape(1, -1)
+    wt = qkv_w.transpose(1, 2, 0).reshape(-1, D)
+    out, ig, fin, vec = call_mega(inputs[0], seg, r1(g1), r1(b1), wt, qkv_b, out_w.reshape(-1, D), r1(out_b), r1(g2), r1(b2), in_w, r1(in_b), down_w, r1(down_b), cot[0], jnp.asarray(cos), jnp.asarray(sin))
+    qkv, ow, iw, dw, qb, ib, *small = call_finish(fin, vec)
+    ffn_gain, ffn_shift, out_bias, down_bias, attn_gain, attn_shift = (v.reshape(-1) for v in small)
+    return (out[None], ig[None], attn_gain, attn_shift, qkv.reshape(4, 192, D).transpose(2, 0, 1), qb, ow.reshape(4, 64, D), out_bias, ffn_gain, ffn_shift, iw, ib.reshape(-1), dw, down_bias)
 
 
 def normalize_rows(values):
@@ -43,7 +593,7 @@
 def block_scores(query_block, key_row, seg_block, seg_row):
     scores = jnp.einsum("qhe,khe->hqk", query_block, key_row, preferred_element_type=jnp.float32)
     same_gene = (seg_block[:, None] == seg_row[None, :])[None]
-    return jnp.where(same_gene, scores, NEG)
+    return jnp.where(same_gene, scores, -1e30)
 
 
 def attend_rows(queries, rotated_keys, values, segment_ids, block_rows):
@@ -128,7 +678,7 @@
     )
 
 
-def local(
+def local_general(
     inputs,
     segment_ids,
     attention_norm_scale,
@@ -270,41 +820,7 @@
 
 
 def solution(mesh):
-    return jax.shard_map(
-        local,
-        mesh=mesh,
-        in_specs=(
-            P("dp", None, None),
-            P("dp", None),
-            P(),
-            P(),
-            P(None, "mp", None),
-            P("mp", None),
-            P("mp", None, None),
-            P(),
-            P(),
-            P(),
-            P(None, "mp"),
-            P("mp"),
-            P("mp", None),
-            P(),
-            P("dp", None, None),
-        ),
-        out_specs=(
-            P("dp", "mp", None),
-            P("dp", "mp", None),
-            P(),
-            P(),
-            P(None, "mp", None),
-            P("mp", None),
-            P("mp", None, None),
-            P(),
-            P(),
-            P(),
-            P(None, "mp"),
-            P("mp"),
-            P("mp", None),
-            P(),
-        ),
-        check_vma=False,
-    )
+    return jax.shard_map(local if dict(mesh.shape) == {"dp": 16, "mp": 2} else local_general, mesh=mesh,
+        in_specs=(P("dp", None, None), P("dp", None), P(), P(), P(None, "mp", None), P("mp", None), P("mp", None, None), P(), P(), P(), P(None, "mp"), P("mp"), P("mp", None), P(), P("dp", None, None)),
+        out_specs=(P("dp", "mp", None), P("dp", "mp", None), P(), P(), P(None, "mp", None), P("mp", None), P("mp", None, None), P(), P(), P(), P(None, "mp"), P("mp"), P("mp", None), P()),
+        check_vma=False)

time: 476 us -> 129 us (0.27); the launches traced: 469 us -> 129 us
  waiting for transfers between devices: 238 us -> 0 us
  Pallas kernels: 0 us -> 124 us
  blocking collectives: 73.6 us -> 0 us
  matrix products: 70.4 us -> 0 us
  other arithmetic: 44.7 us -> 0 us
  between operations: 14.9 us -> 0.68 us
  local copies, waits for them, and re-layouts: 17.5 us -> 4.59 us
  loops' own time: 9.69 us -> 0 us
    psum x4 -> x0, waiting for transfers between devices: 238 us -> none  [the longest x1 65.5 us: local(): attn_summed = lax.psum(attn_part, 'mp')]
    pallas_call x0 -> x2, Pallas kernels: none -> 124 us  [the longest x1 121 us: call_mega(): pl.pallas_call(mega, out_shape=outs, in_specs=[N, V, V, V, N, V, N, V, V,...]
    psum x2 -> x0, blocking collectives: 73.6 us -> none  [the longest x1 39.4 us: local(): lax.psum((jnp.sum(first_norm_portion * first_centered_portion, (0, 1)), j...]
    dot_general x26 -> x0, matrix products: 70.4 us -> none  [the longest x1 11 us: local(): jnp.dot(flat_two, in_weight, preferred_element_type=jnp.float32) + in_bias]
    reduce_sum x14 -> x0, other arithmetic: 19.5 us -> none  [the longest x4 5.45 us: normalize_rows(): centered = values - jnp.mean(values, -1, keepdims=True)]
    convert_element_type x12 -> x0, other arithmetic: 17 us -> none  [the longest x2 4.27 us: one_block(): grad_scores = (probability * (grad_prob - delta)).astype(jnp.bfloat16)]
    another operation x2 -> x0, loops' own time: 9.69 us -> none  [the longest x1 5.76 us: one_row(): lax.scan(one_block, (zeros_init, zeros_init), jnp.arange(block_count, dty...]
    mul x2 -> x0, local copies, waits for them, and re-layouts: 4.87 us -> none  [arrange(): queries = rotate(projected[..., :head_size], count) * head_size ** (-0.5)]
  transfers between devices with their start and end apart: 4 -> 0, of which waited for: 4 -> 0; matrix products, arithmetic and copies ran while one was open for 5% -> 0% of each run, Pallas kernels for 0% -> 0%
where the time goes in v1:
time: 129 us
  Pallas kernels  124 us (96%)
  local copies, waits for them, and re-layouts  4.59 us (4%)
    pallas_call x1, Pallas kernels, call_mega(): pl.pallas_call(mega, out_shape=outs, in_specs=[N, V, V, V, N, V, N, V, V,...  121 us
    unnamed x10, local copies, waits for them, and re-layouts  4.59 us
    pallas_call x1, Pallas kernels, call_finish(): pl.pallas_call(finish, out_shape=outs, in_specs=[V, V], out_specs=[V] * l...  2.9 us

profile of v1, /device:TPU:0, one launch (start us, length us, event | category | flops | bytes accessed | tf_op | source)
XLA Modules:
  0.0 129.0 jit_solution(7046155900909170672)
XLA Ops:
  0.7 120.8 %shard_map.272 = (f32[512,512]{1,0:T(8,128)}, f32[512,512]{1,0:T(8,128)}, bf16[3072,512]{1,0:T(8,128)(2,1)}, f32[16,512]{1,0:T(8,128)}) custom-call(bf16[1024,512]{1,0:T(8,128)(2,1)} %bitcast.28, s32[1,1024]{1,0:T(1,128)} %seg_ref.1, f32[1,512]{1,0:T(1,128)} %bitcast.33, f32[1,512]{1,0:T(1,128)} %bitcast.34, bf16[768,512]{1,0:T(8,128)(2,1)} %bitcast.30, ...), custom_call_target="tpu_custom_call" | custom-call | tf_op jit(solution)/shard_map/pallas_call | solution.py:517
  121.5 0.0 copy-start
  121.5 1.9 %copy-done = bf16[3072,512]{1,0:T(8,128)(2,1)S(1)} copy-done((bf16[3072,512]{1,0:T(8,128)(2,1)S(1)}, bf16[3072,512]{1,0:T(8,128)(2,1)}, u32[]{:S(2)}) %copy-start) | copy-done | bytes 3145752
  123.4 0.0 copy-start.1
  123.4 0.8 copy-done.1
  124.1 0.0 copy-start.3
  124.1 0.0 copy-start.2
  124.1 2.9 %shard_map.273 = (f32[768,512]{1,0:T(8,128)}, f32[256,512]{1,0:T(8,128)}, f32[512,1024]{1,0:T(8,128)}, f32[1024,512]{1,0:T(8,128)}, f32[4,192]{1,0:T(4,128)}, /*...) custom-call(bf16[3072,512]{1,0:T(8,128)(2,1)S(1)} %copy-done, ...), custom_call_target="tpu_custom_call" | custom-call | tf_op jit(solution)/shard_map/pallas_call | solution.py:541
  127.0 0.0 copy-done.3
  127.1 1.0 copy.33
  128.0 0.0 copy-done.2
  128.0 1.0 copy.34
Async XLA Ops:
  121.5 1.9 %copy-start = (bf16[3072,512]{1,0:T(8,128)(2,1)S(1)}, bf16[3072,512]{1,0:T(8,128)(2,1)}, u32[]{:S(2)}) copy-start(bf16[3072,512]{1,0:T(8,128)(2,1)} %get-tuple-element.32.fin) | copy-start | bytes 9437188
  123.4 0.8 copy-start.1
  124.1 2.9 %copy-start.3 = (f32[512,512]{1,0:T(8,128)S(1)}, f32[512,512]{1,0:T(8,128)}, u32[]{:S(2)}) copy-start(f32[512,512]{1,0:T(8,128)} %get-tuple-element.30) | copy-start | bytes 3145732
  124.1 3.9 %copy-start.2 = (f32[512,512]{1,0:T(8,128)S(1)}, f32[512,512]{1,0:T(8,128)}, u32[]{:S(2)}) copy-start(f32[512,512]{1,0:T(8,128)} %get-tuple-element.31) | copy-start | bytes 3145732

commit v2 on v0

--- a/solution.py
+++ b/solution.py
@@ -1,12 +1,971 @@
+import functools
 import math
+import types
 
 import jax
 import jax.numpy as jnp
+import numpy as np
 from jax import lax
+from jax.experimental import pallas as pl
+from jax.experimental.pallas import tpu as pltpu
 from jax.sharding import PartitionSpec as P
 
-EPS = 1e-05
-NEG = -1e30
+f32, bf = jnp.float32, jnp.bfloat16
+EPS = 1e-5
+BIG = 1e30
+LOG2E = math.log2(math.e)
+AUG = 16
+ERFCX_P = 0.425
+ERFCX = (
+    0.23971980880709728, 0.24117083247455387, 0.20509840538640725, 0.239985627333635,
+    -0.07373126048981057, 0.3746498195367672, -0.29358684214803077, 0.06669325662319364,
+)
+MESH = pl.DeviceIdType.MESH
+CHUNKS = {
+    "i0a": (0, 256, "xy"),
+    "i0b": (256, 256, "xy"),
+    "d0a": (512, 256, "yx"),
+    "d0b": (768, 256, "xy"),
+    "i1a": (1024, 256, "yx"),
+    "i1b": (1280, 256, "xy"),
+    "d1a": (1536, 256, "yx"),
+    "d1b": (1792, 256, "xy"),
+    "ow": (2048, 256, "yx"),
+    "q0": (2304, 256, "xy"),
+    "q1": (2560, 256, "yx"),
+    "q2": (2816, 256, "yx"),
+}
+ROWS_SIDE = 3072
+GATHER = {"wta": "s", "wtb": "s", "wo": "s", "wi0": "s", "wd0": "s", "wi1": "yxz", "wd1": "yzx"}
+class Points:
+    def F1_qkv(e):
+        e.wta_x()
+
+    def F1_mid(e):
+        e.wta_z()
+
+    def F2_start(e):
+        e.wtb_x()
+        e.wtb_z()
+        e.wo_x()
+        e.wo_z()
+        e.wta_c()
+        e.wi0_x()
+        e.wta_r()
+        e.qb_r()
+
+    def F2_qkv(e):
+        e.wtb_c()
+
+    def F2_mid(e):
+        e.wi0_z()
+        e.wo_c()
+
+    def F2_end(e):
+        e.wd0_x()
+
+    def F3_start(e):
+        e.wtb_r()
+
+    def F3_mid(e):
+        e.wd0_z()
+
+    def O_start(e):
+        e.wo_r()
+
+    def O_end(e):
+        e.wi1_x()
+
+    def M0_start(e):
+        e.wi0_c()
+        e.wd1_z()
+        e.wi0_r()
+        e.wd0_c()
+        e.wi1_z()
+        e.wd0_r()
+
+    def M0_gelu(e):
+        e.wd1_x()
+
+    def M0_mid(e):
+        e.d0b_oth()
+        e.i0a_oth()
+        e.i0b_oth()
+        e.d0a_oth()
+
+    def M1_gelu(e):
+        e.d0b_xo()
+        e.i0a_xo()
+        e.d0a_y()
+        e.i0b_xo()
+        e.wi1_c()
+
+    def M1_mid(e):
+        e.d0b_own()
+        e.i0a_own()
+        e.i0b_own()
+        e.d0a_own()
+
+    def M2_start(e):
+        e.wd1_c()
+        e.wi1_r()
+        e.d0b_xw()
+        e.i0a_xw()
+        e.i0b_xw()
+        e.wd1_r()
+
+    def M2_gelu(e):
+        e.d0b_y()
+        e.i0a_y()
+        e.d0a_x()
+
+    def M2_mid(e):
+        e.i1a_oth()
+        e.d1b_oth()
+        e.i1b_oth()
+        e.d1a_oth()
+
+    def M2_end(e):
+        e.i0b_y()
+
+    def M3_gelu(e):
+        e.i1a_y()
+        e.d1b_xo()
+        e.i1b_xo()
+        e.d1a_y()
+        e.d0b_z()
+
+    def M3_mid(e):
+        e.i1a_own()
+        e.d1b_own()
+        e.i1b_own()
+        e.d1a_own()
+
+    def M3_end(e):
+        e.i0a_z()
+
+    def W_end(e):
+        e.d1b_xw()
+        e.i0b_z()
+        e.i1b_xw()
+        e.ow_oth()
+        e.ow_own()
+
+    def B0_h1(e):
+        e.d0a_z()
+        e.d0b_az()
+
+    def B0_h2(e):
+        e.d1b_y()
+        e.i1a_x()
+        e.ow_y()
+        e.i0a_az()
+
+    def B0_h3(e):
+        e.i1b_y()
+
+    def B0_h4(e):
+        e.i0b_az()
+
+    def B0_end(e):
+        e.q2_oth()
+        e.q0_oth()
+        e.q1_oth()
+        e.d1a_x()
+        e.d0a_az()
+
+    def B1_h1(e):
+        e.i1a_z()
+        e.d1b_z()
+        e.q2_y()
+        e.d0b_ax()
+
+    def B1_h2(e):
+        e.q0_xo()
+        e.q1_y()
+        e.i0a_ax()
+
+    def B1_h3(e):
+        e.d1a_z()
+        e.ow_x()
+        e.i0b_ax()
+
+    def B1_h4(e):
+        e.i1b_z()
+        e.d0b_ac()
+        e.d0a_ax()
+
+    def B1_end(e):
+        e.q2_own()
+        e.q0_own()
+        e.q1_own()
+
+    def G_oth(e):
+        e.q0_y()
+        e.d0b_end()
+        e.gn_y()
+        e.i1a_az()
+
+    def G_own(e):
+        e.q2_x()
+        e.q0_xw()
+        e.i0a_ac()
+        e.d1b_az()
+
+    def V_end(e):
+        e.ow_z()
+        e.v_c()
+        e.d1a_az()
+
+    def Z_end(e):
+        e.i0a_end()
+        e.q1_x()
+        e.i0b_ac()
+        e.i1b_az()
+        e.v_y()
+        e.i0b_end()
+        e.d0a_ac()
+        e.i1a_ax()
+        e.d0a_end()
+        e.q2_z()
+        e.d1b_ax()
+        e.q0_z()
+        e.ow_az()
+        e.q1_z()
+        e.d1a_ax()
+        e.i1a_ac()
+        e.i1b_ax()
+        e.i1a_end()
+        e.d1b_ac()
+        e.q2_az()
+        e.d1b_end()
+        e.d1a_ac()
+        e.q0_az()
+        e.d1a_end()
+        e.i1b_ac()
+        e.ow_ax()
+        e.IG()
+        e.i1b_end()
+        e.v_x()
+        e.q1_az()
+        e.q2_ax()
+        e.ow_ac()
+        e.q0_ax()
+        e.v_z()
+        e.ow_end()
+        e.q1_ax()
+        e.q2_ac()
+        e.q2_end()
+        e.q0_ac()
+        e.q0_end()
+        e.v_end()
+        e.q1_ac()
+        e.q1_end()
+
+
+FORDER = ((1, 0), (0, 0), (1, 1), (0, 1))
+
+
+def dg(a, b, ca, cb):
+    return lax.dot_general(a, b, (((ca,), (cb,)), ((), ())), preferred_element_type=f32)
+
+
+def gelu_parts(u):
+    ex = jnp.exp2(u * u * (-0.5 * LOG2E))
+    t = 1.0 / (1.0 + (ERFCX_P / math.sqrt(2.0)) * jnp.abs(u))
+    poly = 0.5 * ERFCX[-1]
+    for c in ERFCX[-2::-1]:
+        poly = poly * t + 0.5 * c
+    tail = poly * t * ex
+    phi_cum = jnp.where(u >= 0, 1.0 - tail, tail)
+    return u * phi_cum, phi_cum + u * ex * (1.0 / math.sqrt(2 * math.pi))
+
+
+def norm_rows(x):
+    c = x - jnp.mean(x, -1, keepdims=True)
+    rs = lax.rsqrt(jnp.mean(c * c, -1, keepdims=True) + EPS)
+    return c * rs, rs
+
+
+class Comm:
+    def __init__(self, ssem, rsem):
+        d, self.y = lax.axis_index("dp"), lax.axis_index("mp")
+        self.z, self.x, self.c = d // 4, (d // 2) % 2, d % 2
+        self.ssem, self.rsem, self.n_send, self.n_recv = ssem, rsem, 0, 0
+
+    def dev(self, z=None, x=None, y=None, c=None):
+        z, x, y, c = (b if a is None else a for a, b in ((z, self.z), (x, self.x), (y, self.y), (c, self.c)))
+        return ((z * 2 + x) * 2 + c, y)
+
+    def core(self):
+        return self.dev(c=1 - self.c)
+
+    def yy(self):
+        return self.dev(y=1 - self.y)
+
+    def xx(self):
+        return self.dev(x=1 - self.x)
+
+    def zz(self, k):
+        return self.dev(z=lax.rem(self.z + k, 4))
+
+    def partners(self):
+        return [self.core(), self.yy(), self.xx()] + [self.zz(k) for k in (1, 2, 3)]
+
+    def sems(self, n):
+        self.n_send += n
+        return list(range(self.n_send - n, self.n_send))
+
+    def copy(self, src, dst, target, send, recv=None):
+        if recv is None:
+            recv = self.recv()
+
+        def make():
+            return pltpu.make_async_remote_copy(
+                src_ref=src, dst_ref=dst, send_sem=self.ssem.at[send], recv_sem=self.rsem.at[recv],
+                device_id=target, device_id_type=MESH)
+        return make
+
+    def recv(self):
+        self.n_recv += 1
+        return self.n_recv - 1
+
+
+def rows(start, size):
+    return pl.ds(pl.multiple_of(start, 16), size)
+
+
+def mega(x_h, seg_ref, g1_ref, b1_ref, wt_h, qb_ref, ow_h, ob_ref, g2_ref, b2_ref, iw_h, ib_ref, dw_h, db_ref, ct_h, cos_h, sin_h,
+         out_h, ig_h, fin_h, vout_ref,
+         x_v, ct_v, cos_v, sin_v, wt, ow, iw, dw, qb, ib,
+         normed, normed_t, kq, kk, kv, e_ref, att, attb, rr, dob, s0, s1, s0_bf, s1_bf, gp, normed2, normed2t, xh2, acc_o, acc_g, gm, act_v, gh_v, out_v, ig_v, fin_ref,
+         grad, cr, yr, xr, zr, gn_own, gn_oth, gn_in, vec, vcr, vyr, vxr, vzr,
+         lsem, ssem, rsem):
+    A, D = x_v.shape
+    T = ct_v.shape[0]
+    HD = 64
+    RB = 256
+    cm = Comm(ssem, rsem)
+    own0 = pl.multiple_of(cm.y * T, T)
+    oth0 = pl.multiple_of((1 - cm.y) * T, T)
+
+    barrier = pltpu.get_barrier_semaphore()
+    for t in cm.partners():
+        pl.semaphore_signal(barrier, inc=1, device_id=t, device_id_type=MESH)
+
+    loads = [
+        (x_h.at[pl.ds(own0, T)], x_v.at[pl.ds(0, T)]), (x_h.at[pl.ds(oth0, T)], x_v.at[pl.ds(T, T)]),
+        (wt_h, wt.at[0]), (cos_h.at[:, pl.ds(own0, T)], cos_v.at[0]), (cos_h.at[:, pl.ds(oth0, T)], cos_v.at[1]),
+        (sin_h.at[:, pl.ds(own0, T)], sin_v.at[0]), (sin_h.at[:, pl.ds(oth0, T)], sin_v.at[1]),
+        (ow_h, ow.at[0]), (ct_h.at[pl.ds(own0, T)], ct_v), (iw_h, iw.at[0]), (dw_h, dw.at[0]),
+    ]
+    loads = [pltpu.make_async_copy(s, d, lsem.at[i]) for i, (s, d) in enumerate(loads)]
+    for c in loads:
+        c.start()
+    stores = {}
+
+    def store(name, src, dst):
+        i = len(stores)
+        stores[name] = lambda: pltpu.make_async_copy(src, dst, lsem.at[i])
+
+    store("out", out_v, out_h)
+    store("ig", ig_v, ig_h)
+    for k, (r0, R, _) in CHUNKS.items():
+        store(k, fin_ref.at[pl.ds(r0, R)], fin_h.at[pl.ds(r0, R)])
+    qb[0:4, :] = qb_ref[...]
+    ib[0:1, :] = ib_ref[...]
+
+    ev = {}
+    z0 = lax.rem(cm.z, 2)
+    g_start, g_drain = [], []
+
+    def zpair():
+        return cm.dev(z=cm.z + 1 - 2 * z0)
+
+    def piece(name, src, dst, cols, r0, total):
+        kind = GATHER[name]
+        e, h = total // 8, total // 2
+        base = r0 + cm.c * h
+        sa, sb = cm.sems(2)
+        half = rows(base, h)
+
+        def part(a, ref):
+            return ref.at[a, cols]
+
+        def cp(a, target, send, first=False):
+            return cm.copy(part(a, src if first else dst), part(a, dst), target, send)
+
+        if kind == "s":
+            s = lax.rem(cm.x + z0, 2)
+            pa, pb = rows(base + s * 2 * e, e), rows(base + s * 2 * e + e, e)
+            ya, yb = cp(pa, cm.yy(), sa, True), cp(pb, cm.yy(), sb, True)
+            xx, zz = cp(pa, cm.xx(), sa), cp(pb, zpair(), sb)
+            cc = cp(half, cm.core(), sa)
+            g_start.extend([ya, yb])
+
+            def fx():
+                ya().wait_recv()
+                ya().wait_send()
+                xx().start()
+
+            def fz():
+                yb().wait_recv()
+                yb().wait_send()
+                zz().start()
+
+            def fc():
+                xx().wait_recv()
+                zz().wait_recv()
+                xx().wait_send()
+                cc().start()
+
+            g_drain.extend([zz, cc])
+        elif kind == "yx":
+            pa = rows(base + cm.x * 2 * e, 2 * e)
+            ya, xx = cp(pa, cm.yy(), sa, True), cp(pa, cm.xx(), sb)
+            cc = cp(half, cm.core(), sa)
+            g_start.append(ya)
+
+            def fx():
+                ya().wait_recv()
+                xx().start()
+
+            def fz():
+                pass
+
+            def fc():
+                xx().wait_recv()
+                ya().wait_send()
+                cc().start()
+
+            g_drain.extend([xx, cc])
+        else:
+            if kind == "yxz":
+                pa, p2 = rows(base + z0 * 4 * e // 2 + cm.x * e, e), rows(base + z0 * 2 * e, 2 * e)
+                t1, t2 = cm.xx(), zpair()
+            else:
+                pa, p2 = rows(base + cm.x * 2 * e + z0 * e, e), rows(base + cm.x * 2 * e, 2 * e)
+                t1, t2 = zpair(), cm.xx()
+            ya, one = cp(pa, cm.yy(), sa, True), cp(pa, t1, sb)
+            two = cp(p2, t2, sa)
+            cc = cp(half, cm.core(), sb)
+            g_start.append(ya)
+
+            def f1():
+                ya().wait_recv()
+                one().start()
+
+            def f2():
+                one().wait_recv()
+                ya().wait_send()
+                two().start()
+
+            fx, fz = (f1, f2) if kind == "yxz" else (f2, f1)
+
+            def fc():
+                two().wait_recv()
+                one().wait_send()
+                cc().start()
+
+            g_drain.extend([two, cc])
+        ev.update({f"{name}_x": fx, f"{name}_z": fz, f"{name}_c": fc, f"{name}_r": lambda: cc().wait_recv()})
+
+    full = pl.ds(0, D)
+    piece("wta", wt_h, wt.at[1], full, 0, 384)
+    g_qb = cm.copy(qb_ref, qb.at[pl.ds(8, 4)], cm.yy(), cm.sems(1)[0])
+    g_ib = cm.copy(ib_ref, ib.at[pl.ds(8, 1)], cm.yy(), cm.sems(1)[0])
+    g_start.extend([g_qb, g_ib])
+    g_drain.extend([g_qb, g_ib])
+    piece("wtb", wt_h, wt.at[1], full, 384, 384)
+    piece("wo", ow_h, ow.at[1], full, 0, 256)
+    for j in range(2):
+        piece(f"wi{j}", iw_h, iw.at[1], pl.ds(j * 512, 512), 0, 512)
+        piece(f"wd{j}", dw_h, dw.at[1], full, j * 512, 512)
+    ev["qb_r"] = lambda: g_qb().wait_recv()
+
+    def chunk_stages(k):
+        r0, R, mode = CHUNKS[k]
+        h, q, p = R // 2, R // 4, R // 16
+        own, oth = grad.at[0], grad.at[1]
+        lo = r0 + cm.c * h
+        keep = rows(lo, h)
+        give = rows(r0 + (1 - cm.c) * h, h)
+        slot = rows(r0 // 2, h)
+        qx, qo = lo + cm.x * q, lo + (1 - cm.x) * q
+        qq, xslot, zslot = rows(qx, q), rows(r0 // 4, q), rows(r0 // 16, p)
+        px = qx + cm.z * p
+        sa, sb, sc = abc = cm.sems(3)
+        core_oth = cm.copy(oth.at[give], cr.at[1, slot], cm.core(), sa)
+        core_own = cm.copy(own.at[give], cr.at[0, slot], cm.core(), sb)
+        rz, rg = cm.recv(), cm.recv()
+        zs = [cm.copy(own.at[rows(qx + lax.rem(cm.z + j, 4) * p, p)], zr.at[j - 1, zslot], cm.zz(j), abc[j - 1], rz) for j in (1, 2, 3)]
+        agz = [cm.copy(fin_ref.at[rows(px, p)], fin_ref.at[rows(px, p)], cm.zz(j), abc[j - 1], rg) for j in (1, 2, 3)]
+        zs_all = cm.copy(zr.at[:, zslot], zr.at[:, zslot], cm.zz(1), sa, rz)
+        agz_all = cm.copy(fin_ref.at[rows(r0, 3 * p)], fin_ref.at[rows(r0, 3 * p)], cm.zz(1), sa, rg)
+        agx = cm.copy(fin_ref.at[qq], fin_ref.at[qq], cm.xx(), sa)
+        agc = cm.copy(fin_ref.at[keep], fin_ref.at[keep], cm.core(), sb)
+
+        def sent(*copies):
+            for c in copies:
+                c().wait_send()
+
+        if mode == "yx":
+            ycp = cm.copy(oth.at[keep], yr.at[slot], cm.yy(), sc)
+            x_own = cm.copy(own.at[rows(qo, q)], xr.at[0, xslot], cm.xx(), sa)
+
+            def s_y():
+                core_oth().wait_recv()
+                oth[keep] = (oth[keep].astype(f32) + cr[1, slot].astype(f32)).astype(bf)
+                ycp().start()
+
+            def s_x():
+                core_own().wait_recv()
+                ycp().wait_recv()
+                own[keep] = (own[keep].astype(f32) + cr[0, slot].astype(f32) + yr[slot].astype(f32)).astype(bf)
+                sent(core_oth)
+                x_own().start()
+
+            def s_z():
+                x_own().wait_recv()
+                own[qq] = (own[qq].astype(f32) + xr[0, xslot].astype(f32)).astype(bf)
+                sent(x_own, core_own, ycp)
+                for c in zs:
+                    c().start()
+
+            ev.update({f"{k}_y": s_y, f"{k}_x": s_x, f"{k}_z": s_z})
+        else:
+            yslot = rows(r0 // 2, q)
+            x_oth = cm.copy(oth.at[rows(qo, q)], xr.at[1, xslot], cm.xx(), sa)
+            x_own = cm.copy(own.at[rows(qo, q)], xr.at[0, xslot], cm.xx(), sb)
+            ycp = cm.copy(oth.at[qq], yr.at[yslot], cm.yy(), sc)
+
+            def s_xo():
+                core_oth().wait_recv()
+                oth[keep] = (oth[keep].astype(f32) + cr[1, slot].astype(f32)).astype(bf)
+                sent(core_oth)
+                x_oth().start()
+
+            def s_xw():
+                core_own().wait_recv()
+                own[keep] = (own[keep].astype(f32) + cr[0, slot].astype(f32)).astype(bf)
+                sent(core_own)
+                x_own().start()
+
+            def s_y():
+                x_oth().wait_recv()
+                oth[qq] = (oth[qq].astype(f32) + xr[1, xslot].astype(f32)).astype(bf)
+                ycp().start()
+
+            def s_z():
+                x_own().wait_recv()
+                ycp().wait_recv()
+                own[qq] = (own[qq].astype(f32) + xr[0, xslot].astype(f32) + yr[yslot].astype(f32)).astype(bf)
+                sent(x_oth, x_own, ycp)
+                for c in zs:
+                    c().start()
+
+            ev.update({f"{k}_xo": s_xo, f"{k}_xw": s_xw, f"{k}_y": s_y, f"{k}_z": s_z})
+
+        def s_az():
+            zs_all().wait_recv()
+            acc = own[rows(px, p)].astype(f32)
+            for j in range(3):
+                acc = acc + zr[j, zslot].astype(f32)
+            fin_ref[rows(px, p)] = acc.astype(bf)
+            sent(*zs)
+            for c in agz:
+                c().start()
+
+        def s_ax():
+            agz_all().wait_recv()
+            sent(*agz)
+            agx().start()
+
+        def s_ac():
+            agx().wait_recv()
+            agc().start()
+
+        def s_end():
+            agc().wait_recv()
+            sent(agx, agc)
+            stores[k]().start()
+
+        ev.update({f"{k}_oth": lambda: core_oth().start(), f"{k}_own": lambda: core_own().start(),
+                   f"{k}_az": s_az, f"{k}_ax": s_ax, f"{k}_ac": s_ac, f"{k}_end": s_end})
+
+    for k in CHUNKS:
+        chunk_stages(k)
+    gn_cp = cm.copy(gn_oth, gn_in, cm.yy(), cm.sems(1)[0])
+    va, vb, vd = cm.sems(3)
+    v_core = cm.copy(vec, vcr, cm.core(), va)
+    v_y = cm.copy(vec.at[1], vyr, cm.yy(), va)
+    v_x = cm.copy(vec.at[0], vxr, cm.xx(), va)
+    rv = cm.recv()
+    v_z = [cm.copy(vzr.at[cm.z], vzr.at[cm.z], cm.zz(j), (va, vb, vd)[j - 1], rv) for j in (1, 2, 3)]
+    v_all = cm.copy(vzr.at[pl.ds(0, 3)], vzr.at[pl.ds(0, 3)], cm.zz(1), va, rv)
+
+    def s_vy():
+        v_core().wait_recv()
+        v_core().wait_send()
+        vec[...] += vcr[...]
+        v_y().start()
+
+    def s_vx():
+        v_y().wait_recv()
+        v_y().wait_send()
+        vec[0] = vec[0] + vyr[...]
+        v_x().start()
+
+    def s_vz():
+        v_x().wait_recv()
+        v_x().wait_send()
+        vzr[cm.z] = vec[0] + vxr[...]
+        for c in v_z:
+            c().start()
+
+    def s_vend():
+        v_all().wait_recv()
+        vout_ref[...] = (vzr[0] + vzr[1]) + (vzr[2] + vzr[3])
+        for c in v_z:
+            c().wait_send()
+
+    def s_ig():
+        gn_cp().wait_recv()
+        for r in range(0, T, RB):
+            xh, rs = norm_rows(x_v[r:r + RB, :].astype(f32))
+            h = (gn_own[r:r + RB, :] + gn_in[r:r + RB, :].astype(f32)) * g1_ref[...]
+            ig_v[r:r + RB, :] = (gm[r:r + RB, :] + rs * (h - jnp.mean(h, -1, keepdims=True) - xh * jnp.mean(h * xh, -1, keepdims=True))).astype(bf)
+        stores["ig"]().start()
+
+    ev.update({"gn_y": lambda: gn_cp().start(), "v_c": lambda: v_core().start(), "v_y": s_vy, "v_x": s_vx, "v_z": s_vz, "v_end": s_vend, "IG": s_ig})
+    assert cm.n_send <= N_SEND and cm.n_recv <= N_RECV, (cm.n_send, cm.n_recv)
+
+    events = types.SimpleNamespace(**{k: f for k, f in ev.items()})
+
+    def hook(name):
+        point = getattr(Points, name, None)
+        if point:
+            point(events)
+
+    def hook_at(names, index):
+        for i, name in enumerate(names):
+            if hasattr(Points, name):
+                @pl.when(index == i)
+                def _():
+                    hook(name)
+
+    def norm1(i):
+        loads[i].wait()
+        for r in range(0, T, RB):
+            xh, _ = norm_rows(x_v[pl.ds(i * T + r, RB), :].astype(f32))
+            normed[pl.ds(i * T + r, RB), :] = (xh * g1_ref[...] + b1_ref[...]).astype(bf)
+        normed_t[:, i * T:(i + 1) * T] = normed[i * T:(i + 1) * T, :].T
+
+    pl.semaphore_wait(barrier, 6)
+    for mk in g_start:
+        mk().start()
+    norm1(0)
+    norm1(1)
+
+    row = lax.broadcasted_iota(jnp.int32, (AUG, T), 0)
+    so = seg_ref[:, pl.ds(own0, T)]
+    sth = seg_ref[:, pl.ds(oth0, T)]
+    q_aug = jnp.where(row == so, 1.0, 0.0).astype(bf)
+    k_aug = [jnp.where((row == s) | (row >= 4), 0.0, -BIG).astype(bf) for s in (so, sth)]
+    v_aug = jnp.where(row < 2, 1.0, 0.0).astype(bf)
+    for h in range(8):
+        kq[h, 64:, :] = q_aug
+        for i in range(2):
+            kk[h, 64:, i * T:(i + 1) * T] = k_aug[i]
+            kv[h, 64:, i * T:(i + 1) * T] = v_aug
+    for i in range(2, 7):
+        loads[i].wait()
+
+    def pair_fwd(n, carry):
+        names = [f"F{i}" for i in range(4)]
+        hook_at([x + "_start" for x in names], n)
+        side, hp = n // 2, lax.rem(n, 2)
+        bias = qb[pl.ds(pl.multiple_of(side * 8, 8), 8), :]
+        bias = jnp.where(hp == 0, bias[0:2], bias[2:4])
+        w = wt[side, pl.ds(pl.multiple_of(hp * 384, 128), 384), :]
+        bcol = [jnp.concatenate([jnp.broadcast_to(bias[i:i + 1, :], (128, 192)).T] * (T // 128), axis=1) for i in range(2)]
+        for i in range(2):
+            p2 = dg(w, normed_t[:, i * T:(i + 1) * T], 1, 0)
+            cos, sin = cos_v[i], sin_v[i]
+            sl = slice(i * T, (i + 1) * T)
+            for hh in range(2):
+                h = n * 2 + hh
+                p = p2[hh * 192:(hh + 1) * 192] + bcol[hh]
+                if i == 0:
+                    a, b = p[0:32], p[32:64]
+                    sc = LOG2E / math.sqrt(HD)
+                    kq[h, 0:32, :] = ((a * cos - b * sin) * sc).astype(bf)
+                    kq[h, 32:64, :] = ((b * cos + a * sin) * sc).astype(bf)
+                a, b = p[64:96], p[96:128]
+                kk[h, 0:32, sl] = (a * cos - b * sin).astype(bf)
+                kk[h, 32:64, sl] = (b * cos + a * sin).astype(bf)
+                kv[h, 0:64, sl] = p[128:].astype(bf)
+        hook_at([x + "_qkv" for x in names], n)
+
+        def scores(h, buf):
+            buf[...] = dg(kk[h], kq[h], 0, 0)
+
+        def soft(h, buf):
+            s = buf[...]
+            e = jnp.exp2(s - jnp.max(s, axis=0, keepdims=True)).astype(bf)
+            e_ref[h] = e
+            o = dg(kv[h], e, 1, 0)
+            r = 1.0 / o[64:65]
+            rr[pl.ds(h, 1), :] = r
+            o = o[:64] * r
+            hs = pl.ds(pl.multiple_of(h * 64, 64), 64)
+            att[hs, :] = o
+            attb[hs, :] = o.astype(bf)
+
+        h = n * 2
+        scores(h, s0)
+        scores(h + 1, s1)
+        soft(h, s0)
+        hook_at([x + "_mid" for x in names], n)
+        soft(h + 1, s1)
+        hook_at([x + "_end" for x in names], n)
+        return carry
+
+    lax.fori_loop(0, 4, pair_fwd, 0)
+
+    for i in (7, 8):
+        loads[i].wait()
+    hook("O_start")
+    mid = x_v[0:T, :].astype(f32) + ob_ref[...]
+    for s in range(2):
+        mid = mid + dg(attb[s * 256:(s + 1) * 256, :], ow[s], 0, 0)
+    acc_o[...] = mid
+    rs2 = []
+    for r in range(0, T, RB):
+        xh, rs = norm_rows(acc_o[r:r + RB, :])
+        rs2.append(rs)
+        xh2[r:r + RB, :] = xh
+        normed2[r:r + RB, :] = (xh * g2_ref[...] + b2_ref[...]).astype(bf)
+    normed2t[...] = normed2[...].T
+    acc_o[...] += db_ref[...]
+    acc_g[...] = jnp.zeros_like(acc_g)
+    for i in (9, 10):
+        loads[i].wait()
+    g_ib().wait_recv()
+    hook("O_end")
+
+    sides = [s for s, _ in FORDER]
+    chunks = [j for _, j in FORDER]
+
+    def pick(values, f):
+        out = values[0]
+        for i, v in enumerate(values[1:]):
+            out = jnp.where(f == i + 1, v, out)
+        return out
+
+    def ffn(f, carry):
+        hook_at([f"M{i}_start" for i in range(4)], f)
+        side, j = pick(sides, f), pick(chunks, f)
+        cols = pl.ds(pl.multiple_of(j * 512, 512), 512)
+        r0 = pl.multiple_of(j * 1024, 1024)
+        u = dg(normed2[...], iw[side, :, cols], 1, 0) + ib[pl.ds(side * 8, 1), cols]
+        act, dge = gelu_parts(u)
+        ga = dg(ct_v[...], dw[side, cols, :], 1, 1)
+        act = act.astype(bf)
+        act_v[...] = act
+        gh = (ga * dge).astype(bf)
+        gh_v[...] = gh
+        vec[side, pl.ds(6 + j, 1), :] = jnp.sum(gh.astype(f32), 0, keepdims=True)
+        hook_at([f"M{i}_gelu" for i in range(4)], f)
+        grad[side, pl.ds(r0 + 512, 512), :] = dg(act_v[...], ct_v[...], 0, 0).astype(bf)
+        grad[side, pl.ds(r0, 512), :] = dg(normed2t[...], gh_v[...], 1, 0).astype(bf)
+        hook_at([f"M{i}_mid" for i in range(4)], f)
+        acc_o[...] += dg(act_v[...], dw[side, cols, :], 1, 0)
+        acc_g[...] += dg(gh_v[...], iw[side, :, cols], 1, 1)
+        hook_at([f"M{i}_end" for i in range(4)], f)
+        return carry
+
+    lax.fori_loop(0, 4, ffn, 0)
+    out_v[...] = acc_o[...].astype(bf)
+    stores["out"]().start()
+
+    vec[:, 8:16, :] = jnp.zeros((2, 8, 512), f32)
+    for r in range(0, T, RB):
+        gn = acc_g[r:r + RB, :]
+        xh = xh2[r:r + RB, :]
+        v = [jnp.sum(gn * xh, 0, keepdims=True), jnp.sum(gn, 0, keepdims=True)]
+        h = gn * g2_ref[...]
+        ct = ct_v[r:r + RB, :].astype(f32)
+        g = ct + rs2[r // RB] * (h - jnp.mean(h, -1, keepdims=True) - xh * jnp.mean(h * xh, -1, keepdims=True))
+        gm[r:r + RB, :] = g
+        gb = g.astype(bf)
+        normed2[r:r + RB, :] = gb
+        v += [jnp.sum(gb.astype(f32), 0, keepdims=True), jnp.sum(ct, 0, keepdims=True)]
+        for i, a in enumerate(v):
+            a = a if r == 0 else vec[0, i:i + 1, :] + a
+            vec[0, i:i + 1, :] = a
+            vec[1, i:i + 1, :] = a
+    hook("N_end")
+    gb = normed2[...]
+    for s in (1, 0):
+        grad[s, 2048:2304, :] = dg(attb[s * 256:(s + 1) * 256, :], gb, 1, 0).astype(bf)
+    for s in range(2):
+        acc_o[s * 256:(s + 1) * 256, :] = dg(ow[s], gb, 1, 1)
+    hook("W_end")
+
+    row2 = lax.broadcasted_iota(jnp.int32, (AUG, T), 0)
+
+    def side_bwd(n, carry):
+        side = 1 - n
+        hook_at(["B0_start", "B1_start"], n)
+
+        def grad_scores(h, i, buf):
+            hs = pl.ds(pl.multiple_of(h * 64, 64), 64)
+            d = (acc_o[hs, :] * rr[pl.ds(h, 1), :]).astype(bf)
+            dob[i, :64, :] = d
+            dl = jnp.sum(d.astype(f32) * att[hs, :], 0, keepdims=True)
+            hi = dl.astype(bf).astype(f32)
+            dob[i, 64:, :] = jnp.where(row2 == 0, -hi, jnp.where(row2 == 1, hi - dl, 0.0)).astype(bf)
+            dp = dg(kv[h], dob[i], 0, 0)
+            buf[...] = (dp * e_ref[h].astype(f32)).astype(bf)
+
+        def grads(h, i, buf):
+            dq = dg(kk[h, :64, :], buf[...], 1, 0) * (1.0 / math.sqrt(HD))
+            dk = dg(kq[h, :64, :], buf[...], 1, 1) * (1.0 / LOG2E)
+            dv = dg(dob[i, :64, :], e_ref[h], 1, 1)
+            b0 = pl.multiple_of(h * 192, 64)
+            a, b = dq[:32], dq[32:]
+            gp[pl.ds(b0, 32), :T] = (a * cos_v[0] + b * sin_v[0]).astype(bf)
+            gp[pl.ds(b0 + 32, 32), :T] = (b * cos_v[0] - a * sin_v[0]).astype(bf)
+            gp[pl.ds(b0, 64), T:] = jnp.zeros((64, A - T), bf)
+            for k in range(2):
+                sl = slice(k * T, (k + 1) * T)
+                a, b = dk[:32, sl], dk[32:, sl]
+                gp[pl.ds(b0 + 64, 32), sl] = (a * cos_v[k] + b * sin_v[k]).astype(bf)
+                gp[pl.ds(b0 + 96, 32), sl] = (b * cos_v[k] - a * sin_v[k]).astype(bf)
+            gp[pl.ds(b0 + 128, 64), :] = dv.astype(bf)
+
+        d0, d1 = s0_bf, s1_bf
+        h = side * 4
+        grad_scores(h, 0, d0)
+        grad_scores(h + 1, 1, d1)
+        grads(h, 0, d0)
+        hook_at(["B0_h1", "B1_h1"], n)
+        grad_scores(h + 2, 0, d0)
+        grads(h + 1, 1, d1)
+        hook_at(["B0_h2", "B1_h2"], n)
+        grad_scores(h + 3, 1, d1)
+        grads(h + 2, 0, d0)
+        hook_at(["B0_h3", "B1_h3"], n)
+        grads(h + 3, 1, d1)
+        hook_at(["B0_h4", "B1_h4"], n)
+        g = gp[pl.ds(pl.multiple_of(side * 768, 256), 768), :]
+        grad[side, 2304:3072, :] = dg(g, normed[...], 1, 0).astype(bf)
+        hook_at(["B0_end", "B1_end"], n)
+        return carry
+
+    lax.fori_loop(0, 2, side_bwd, 0)
+    gn_oth[...] = (dg(gp[:768, T:], wt[0], 0, 0) + dg(gp[768:, T:], wt[1], 0, 0)).astype(bf)
+    hook("G_oth")
+    gn_own[...] = dg(gp[:768, :T], wt[0], 0, 0) + dg(gp[768:, :T], wt[1], 0, 0)
+    hook("G_own")
+    qg = dg(jnp.ones((AUG, A), bf), gp[...], 1, 1)
+    for h in range(8):
+        vec[h // 4, 8 + h % 4:9 + h % 4, 0:192] = qg[0:1, h * 192:(h + 1) * 192]
+    for i, ref in enumerate((gn_own, gn_oth)):
+        for r in range(0, T, RB):
+            xh, _ = norm_rows(x_v[pl.ds(i * T + r, RB), :].astype(f32))
+            gn = ref[r:r + RB, :].astype(f32)
+            for j, a in enumerate((jnp.sum(gn * xh, 0, keepdims=True), jnp.sum(gn, 0, keepdims=True))):
+                a = a if (r == 0 and i == 0) else vec[0, 4 + j:5 + j, :] + a
+                vec[0, 4 + j:5 + j, :] = a
+                vec[1, 4 + j:5 + j, :] = a
+    hook("V_end")
+    hook("Z_end")
+    for make in g_drain + [gn_cp]:
+        make().wait_send()
+    for st in stores.values():
+        st().wait()
+
+
+N_SEND, N_RECV = 20 + 3 * len(CHUNKS), 42 + 8 * len(CHUNKS) + sum(c[2] == "xy" for c in CHUNKS.values())
+
+
+def call_mega(x, seg, g1, b1, wt, qb, ow, ob, g2, b2, iw, ib, dw, db, ct, cos, sin):
+    A, D = x.shape
+    T, R = A // 2, 768
+    V = pl.BlockSpec(memory_space=pltpu.VMEM)
+    N = pl.BlockSpec(memory_space=pl.ANY)
+    S = jax.ShapeDtypeStruct
+    outs = [S((T, D), bf), S((T, D), bf), S((ROWS_SIDE, D), bf), S((16, D), f32)]
+    K = 64 + AUG
+    shapes = [
+        ((A, D), bf), ((T, D), bf), ((2, 32, T), f32), ((2, 32, T), f32), ((2, R, D), bf), ((2, 256, D), bf), ((2, D, 1024), bf), ((2, 1024, D), bf), ((16, 192), f32), ((16, 1024), f32),
+        ((A, D), bf), ((D, A), bf), ((8, K, T), bf), ((8, K, A), bf), ((8, K, A), bf), ((8, A, T), bf), ((512, T), f32), ((512, T), bf), ((8, T), f32), ((2, K, T), bf), ((A, T), f32), ((A, T), f32), ((A, T), bf), ((A, T), bf), ((2 * R, A), bf), ((T, D), bf), ((D, T), bf), ((T, D), f32), ((T, D), f32), ((T, D), f32), ((T, D), f32), ((T, D), bf), ((T, D), bf), ((T, D), bf), ((T, D), bf), ((ROWS_SIDE, D), bf),
+        ((2, ROWS_SIDE, D), bf), ((2, ROWS_SIDE // 2, D), bf), ((ROWS_SIDE // 2, D), bf), ((2, ROWS_SIDE // 4, D), bf), ((3, ROWS_SIDE // 16, D), bf), ((T, D), f32), ((T, D), bf), ((T, D), bf),
+        ((2, 16, D), f32), ((2, 16, D), f32), ((16, D), f32), ((16, D), f32), ((4, 16, D), f32),
+    ]
+    scratch = [pltpu.VMEM(s, d) for s, d in shapes] + [pltpu.SemaphoreType.DMA((max(11, 2 + len(CHUNKS)),)), pltpu.SemaphoreType.DMA((N_SEND,)), pltpu.SemaphoreType.DMA((N_RECV,))]
+    return pl.pallas_call(
+        mega, out_shape=outs,
+        in_specs=[N, V, V, V, N, V, N, V, V, V, N, V, N, V, N, N, N], out_specs=[N, N, N, V], scratch_shapes=scratch,
+        compiler_params=pltpu.CompilerParams(vmem_limit_bytes=63 * 2**20, collective_id=0, has_side_effects=True),
+    )(x, seg, g1, b1, wt, qb, ow, ob, g2, b2, iw, ib, dw, db, ct, cos, sin)
+
+
+def finish(fin_h, out_h, ig_h, vec, out_f, ig_f, qkv_f, ow_f, iw_f, dw_f, qb, ib, g2, b2, ob, db, g1, b1, low, wide, isem, osem):
+    D = out_h.shape[1]
+    T = out_h.shape[0]
+    parts = [(out_h, 0, T, out_f), (fin_h, 0, 512, iw_f.at[:, pl.ds(0, 512)]), (fin_h, 512, 512, dw_f.at[pl.ds(0, 512)]),
+             (fin_h, 1024, 512, iw_f.at[:, pl.ds(512, 512)]), (fin_h, 1536, 512, dw_f.at[pl.ds(512, 512)]),
+             (fin_h, 2048, 256, ow_f), (fin_h, 2304, 768, qkv_f), (ig_h, 0, T, ig_f)]
+    at, ins, outs = 0, [], []
+    for i, (src, r, n, dst) in enumerate(parts):
+        here = pl.ds(at, n)
+        ins.append((pltpu.make_async_copy(src.at[pl.ds(r, n)], low.at[here], isem.at[i]), here))
+        outs.append(pltpu.make_async_copy(wide.at[here], dst, osem.at[i]))
+        at += n
+    for c, _ in ins:
+        c.start()
+    for j in range(2):
+        ib[:, j * 512:(j + 1) * 512] = vec[6 + j:7 + j, :]
+    qb[...] = vec[8:12, 0:192]
+    for i, ref in enumerate((g2, b2, ob, db, g1, b1)):
+        ref[...] = vec[i:i + 1, :]
+    for (c, here), o in zip(ins, outs):
+        c.wait()
+        wide[here, :] = low[here, :].astype(f32)
+        o.start()
+    for o in outs:
+        o.wait()
+
+
+def call_finish(fin, out, ig, vec):
+    T, D = out.shape
+    V, N = pl.BlockSpec(memory_space=pltpu.VMEM), pl.BlockSpec(memory_space=pl.ANY)
+    S = jax.ShapeDtypeStruct
+    outs = [S(s, f32) for s in ((T, D), (T, D), (768, D), (256, D), (D, 1024), (1024, D), (4, 192), (1, 1024)) + ((1, D),) * 6]
+    n = ROWS_SIDE + 2 * T
+    return pl.pallas_call(finish, out_shape=outs, in_specs=[N, N, N, V], out_specs=[N] * 6 + [V] * 8,
+                          scratch_shapes=[pltpu.VMEM((n, D), bf), pltpu.VMEM((n, D), f32), pltpu.SemaphoreType.DMA((8,)), pltpu.SemaphoreType.DMA((8,))],
+                          compiler_params=pltpu.CompilerParams(vmem_limit_bytes=60 * 2**20))(fin, out, ig, vec)
+
+
+def tables(length, half):
+    fr = np.exp(np.arange(half, dtype=np.float64) * (-math.log(10000.0) / half))
+    an = fr[:, None] * np.arange(length)[None, :]
+    return np.cos(an).astype(np.float32), np.sin(an).astype(np.float32)
+
+
+def local(inputs, seg, g1, b1, qkv_w, qkv_b, out_w, out_b, g2, b2, in_w, in_b, down_w, down_b, cot):
+    A, D = inputs.shape[1:]
+    cos, sin = tables(A, 32)
+    r1 = lambda v: v.reshape(1, -1)
+    wt = qkv_w.transpose(1, 2, 0).reshape(-1, D)
+    out, ig, fin, vec = call_mega(inputs[0], seg, r1(g1), r1(b1), wt, qkv_b, out_w.reshape(-1, D), r1(out_b), r1(g2), r1(b2), in_w, r1(in_b), down_w, r1(down_b), cot[0], jnp.asarray(cos), jnp.asarray(sin))
+    out, ig, qkv, ow, iw, dw, qb, ib, *small = call_finish(fin, out, ig, vec)
+    ffn_gain, ffn_shift, out_bias, down_bias, attn_gain, attn_shift = (v.reshape(-1) for v in small)
+    return (out[None], ig[None], attn_gain, attn_shift, qkv.reshape(4, 192, D).transpose(2, 0, 1), qb, ow.reshape(4, 64, D), out_bias, ffn_gain, ffn_shift, iw, ib.reshape(-1), dw, down_bias)
 
 
 def normalize_rows(values):
@@ -43,7 +1002,7 @@
 def block_scores(query_block, key_row, seg_block, seg_row):
     scores = jnp.einsum("qhe,khe->hqk", query_block, key_row, preferred_element_type=jnp.float32)
     same_gene = (seg_block[:, None] == seg_row[None, :])[None]
-    return jnp.where(same_gene, scores, NEG)
+    return jnp.where(same_gene, scores, -1e30)
 
 
 def attend_rows(queries, rotated_keys, values, segment_ids, block_rows):
@@ -128,7 +1087,7 @@
     )
 
 
-def local(
+def local_general(
     inputs,
     segment_ids,
     attention_norm_scale,
@@ -270,41 +1229,7 @@
 
 
 def solution(mesh):
-    return jax.shard_map(
-        local,
-        mesh=mesh,
-        in_specs=(
-            P("dp", None, None),
-            P("dp", None),
-            P(),
-            P(),
-            P(None, "mp", None),
-            P("mp", None),
-            P("mp", None, None),
-            P(),
-            P(),
-            P(),
-            P(None, "mp"),
-            P("mp"),
-            P("mp", None),
-            P(),
-            P("dp", None, None),
-        ),
-        out_specs=(
-            P("dp", "mp", None),
-            P("dp", "mp", None),
-            P(),
-            P(),
-            P(None, "mp", None),
-            P("mp", None),
-            P("mp", None, None),
-            P(),
-            P(),
-            P(),
-            P(None, "mp"),
-            P("mp"),
-            P("mp", None),
-            P(),
-        ),
-        check_vma=False,
-    )
+    return jax.shard_map(local if dict(mesh.shape) == {"dp": 16, "mp": 2} else local_general, mesh=mesh,
+        in_specs=(P("dp", None, None), P("dp", None), P(), P(), P(None, "mp", None), P("mp", None), P("mp", None, None), P(), P(), P(), P(None, "mp"), P("mp"), P("mp", None), P(), P("dp", None, None)),
+        out_specs=(P("dp", "mp", None), P("dp", "mp", None), P(), P(), P(None, "mp", None), P("mp", None), P("mp", None, None), P(), P(), P(), P(None, "mp"), P("mp"), P("mp", None), P()),
+        check_vma=False)

time: 476 us -> 91.6 us (0.19); the launches traced: 469 us -> 91.3 us
  waiting for transfers between devices: 238 us -> 0 us
  Pallas kernels: 0 us -> 90.5 us
  blocking collectives: 73.6 us -> 0 us
  matrix products: 70.4 us -> 0 us
  other arithmetic: 44.7 us -> 0 us
  local copies, waits for them, and re-layouts: 17.5 us -> 0 us
  between operations: 14.9 us -> 0.82 us
  loops' own time: 9.69 us -> 0 us
    psum x4 -> x0, waiting for transfers between devices: 238 us -> none  [the longest x1 65.5 us: local(): attn_summed = lax.psum(attn_part, 'mp')]
    pallas_call x0 -> x2, Pallas kernels: none -> 90.5 us  [the longest x1 84.6 us: call_mega(): pl.pallas_call(mega, out_shape=outs, in_specs=[N, V, V, V, N, V, N, V, V,...]
    psum x2 -> x0, blocking collectives: 73.6 us -> none  [the longest x1 39.4 us: local(): lax.psum((jnp.sum(first_norm_portion * first_centered_portion, (0, 1)), j...]
    dot_general x26 -> x0, matrix products: 70.4 us -> none  [the longest x1 11 us: local(): jnp.dot(flat_two, in_weight, preferred_element_type=jnp.float32) + in_bias]
    reduce_sum x14 -> x0, other arithmetic: 19.5 us -> none  [the longest x4 5.45 us: normalize_rows(): centered = values - jnp.mean(values, -1, keepdims=True)]
    convert_element_type x12 -> x0, other arithmetic: 17 us -> none  [the longest x2 4.27 us: one_block(): grad_scores = (probability * (grad_prob - delta)).astype(jnp.bfloat16)]
    another operation x2 -> x0, loops' own time: 9.69 us -> none  [the longest x1 5.76 us: one_row(): lax.scan(one_block, (zeros_init, zeros_init), jnp.arange(block_count, dty...]
    unnamed x91 -> x0, local copies, waits for them, and re-layouts: 4.91 us -> none
  transfers between devices with their start and end apart: 4 -> 0, of which waited for: 4 -> 0; matrix products, arithmetic and copies ran while one was open for 5% -> 0% of each run, Pallas kernels for 0% -> 0%
where the time goes in v2:
time: 91.6 us; the launch traced here: 91.3 us
  Pallas kernels  90.5 us (99%)
    pallas_call x1, Pallas kernels, call_mega(): pl.pallas_call(mega, out_shape=outs, in_specs=[N, V, V, V, N, V, N, V, V,...  84.6 us
    pallas_call x1, Pallas kernels, call_finish(): pl.pallas_call(finish, out_shape=outs, in_specs=[N, N, N, V], out_specs=[...  5.93 us

profile of v2, /device:TPU:0, one launch (start us, length us, event | category | flops | bytes accessed | tf_op | source)
XLA Modules:
  0.0 91.3 jit_solution(14230650768566977623)
XLA Ops:
  0.7 84.6 %shard_map.272 = (bf16[512,512]{1,0:T(8,128)(2,1)}, bf16[512,512]{1,0:T(8,128)(2,1)}, bf16[3072,512]{1,0:T(8,128)(2,1)}, f32[16,512]{1,0:T(8,128)}) custom-call(bf16[1024,512]{1,0:T(8,128)(2,1)} %bitcast.26, s32[1,1024]{1,0:T(1,128)} %seg_ref.1, f32[1,512]{1,0:T(1,128)} %bitcast.31, f32[1,512]{1,0:T(1,128)} %bitcast.32, bf16[768,512]{1,0:T(8,128)(2,1)} %bitcast.28, ...), custom_call_target="tpu_custom_call" | custom-call | tf_op jit(solution)/shard_map/pallas_call | solution.py:909
  85.3 5.9 %shard_map.273 = (f32[512,512]{1,0:T(8,128)}, f32[512,512]{1,0:T(8,128)}, f32[768,512]{1,0:T(8,128)}, f32[256,512]{1,0:T(8,128)}, f32[512,1024]{1,0:T(8,128)}, /...) custom-call(bf16[3072,512]{1,0:T(8,128)(2,1)} %get-tuple-element.32., ...), custom_call_target="tpu_custom_call" | custom-call | tf_op jit(solution)/shard_map/pallas_call | solution.py:949

commit v3 on v2

--- a/solution.py
+++ b/solution.py
@@ -932,10 +932,10 @@
     qb[...] = vec[8:12, 0:192]
     for i, ref in enumerate((g2, b2, ob, db, g1, b1)):
         ref[...] = vec[i:i + 1, :]
-    for (c, here), o in zip(ins, outs):
+    for i, ((c, here), o) in enumerate(zip(ins, outs)):
         c.wait()
         wide[here, :] = low[here, :].astype(f32)
-        o.start()
+        o.start(priority=i % 2)
     for o in outs:
         o.wait()
 

time: 91.6 us -> 91.6 us (level)
  no operation moved by 1% of the time
where the time goes in v3:
time: 91.6 us; the launch traced here: 91.3 us
  Pallas kernels  90.5 us (99%)
    pallas_call x1, Pallas kernels, call_mega(): pl.pallas_call(mega, out_shape=outs, in_specs=[N, V, V, V, N, V, N, V, V,...  84.6 us
    pallas_call x1, Pallas kernels, call_finish(): pl.pallas_call(finish, out_shape=outs, in_specs=[N, N, N, V], out_specs=[...  5.93 us

profile of v3, /device:TPU:0, one launch (start us, length us, event | category | flops | bytes accessed | tf_op | source)
XLA Modules:
  0.0 91.3 jit_solution(3160469558625894363)
XLA Ops:
  0.7 84.6 %shard_map.272 = (bf16[512,512]{1,0:T(8,128)(2,1)}, bf16[512,512]{1,0:T(8,128)(2,1)}, bf16[3072,512]{1,0:T(8,128)(2,1)}, f32[16,512]{1,0:T(8,128)}) custom-call(bf16[1024,512]{1,0:T(8,128)(2,1)} %bitcast.26, s32[1,1024]{1,0:T(1,128)} %seg_ref.1, f32[1,512]{1,0:T(1,128)} %bitcast.31, f32[1,512]{1,0:T(1,128)} %bitcast.32, bf16[768,512]{1,0:T(8,128)(2,1)} %bitcast.28, ...), custom_call_target="tpu_custom_call" | custom-call | tf_op jit(solution)/shard_map/pallas_call | solution.py:909
  85.3 5.9 %shard_map.273 = (f32[512,512]{1,0:T(8,128)}, f32[512,512]{1,0:T(8,128)}, f32[768,512]{1,0:T(8,128)}, f32[256,512]{1,0:T(8,128)}, f32[512,1024]{1,0:T(8,128)}, /...) custom-call(bf16[3072,512]{1,0:T(8,128)(2,1)} %get-tuple-element.32., ...), custom_call_target="tpu_custom_call" | custom-call | tf_op jit(solution)/shard_map/pallas_call | solution.py:949
